TPU v7x, 32 devices: a whole 2x2x4 slice. The times are simulated.
32 devices in a mesh: chan: 8 (over z, y), tm: 4 (over x, core).
Axes of the slice: x: 2, y: 2, z: 4, core: 2. Of those that a mesh axis runs over, the one named last changes fastest.
Arguments:
- voltages: bfloat16 [2048, 524288], P('chan', 'tm'), may hold values from -6 to 6
- taps: float32 [8, 8192], replicated, may hold values from -2 to 2
- flags: int32 [2048, 64], P('chan', 'tm'), may hold values 0 or 1
- offsets: int32 [8], P('chan'), may hold values from 0 to 7
Outputs:
- visibilities: bfloat16 [8, 2048, 2, 2048], P('chan', 'tm')
All inputs are finite; a program needn't handle non-finite values. No bound on the sum of `flags` on one device may be relied on, other than what follows from the above.
Results may differ from a plain program's by a relative error of at most 0.0058.
Values may be sent and summed in bfloat16 or wider, within the bound.
No kernel may reach another device: no remote copies, remote signals or barrier semaphores. Data moves between devices by JAX's collectives and lax.ppermute only.
A program may use at most 384 MiB of HBM per device.

v0:
```python
import math

import jax
import jax.numpy as jnp
from jax import lax
from jax.sharding import PartitionSpec as P

TAPS = 8


def from_behind(block, axis, distance):
    devices = range(lax.axis_size(axis))
    route = [(i - distance, i) for i in devices if i - distance in devices]
    return lax.ppermute(block, axis, route)


def channel_table(frame, channels, zero_shift):
    samples = jnp.arange(frame, dtype=jnp.int32) + zero_shift
    numbers = jnp.arange(channels, dtype=jnp.int32) * (frame // (2 * channels)) + frame // (
        4 * channels
    )
    phase = samples[:, None] * numbers[None, :] % frame
    angle = phase.astype(jnp.float32) * (2.0 * math.pi / frame)
    norm_scale = 1.0 / math.sqrt(frame)
    return jnp.stack([jnp.cos(angle) * norm_scale, -jnp.sin(angle) * norm_scale], axis=2)


def filter_frames(extended, taps, frame_count):
    history = taps.shape[0] - 1
    total = jnp.zeros((extended.shape[0], frame_count, extended.shape[2]), jnp.float32)
    for tap_index in range(taps.shape[0]):
        begin = history - tap_index
        total = total + taps[tap_index][None, None, :] * extended[
            :, begin : begin + frame_count, :
        ].astype(jnp.float32)
    return total


def transform(dft_table, weighted):
    return jnp.einsum("nkr,isn->krsi", dft_table, weighted, precision=lax.Precision.HIGHEST)


def build_columns(real_part, imag_part, rotation):
    rolled_real = jnp.roll(real_part, -rotation, axis=1)
    rolled_imag = jnp.roll(imag_part, -rotation, axis=1)
    first = jnp.concatenate([rolled_real, rolled_imag], axis=0)
    second = jnp.concatenate([-rolled_imag, rolled_real], axis=0)
    return jnp.stack([first, second], axis=1)


def products(row_side, col_side):
    width = col_side.shape[2]
    flat = col_side.reshape(col_side.shape[0], 2 * width)
    result = jnp.dot(row_side.T, flat, preferred_element_type=jnp.float32)
    return result.reshape(row_side.shape[1], 2, width)


def shards(voltages, taps, flags, offsets):
    chan_count = lax.axis_size("chan")
    time_count = lax.axis_size("tm")
    local_inputs = voltages.shape[0]
    spec_local = flags.shape[1]
    frame = voltages.shape[1] // spec_local
    history = TAPS - 1
    zero_shift = jnp.minimum(offsets[0], 0)
    dft_table = channel_table(frame, chan_count, zero_shift)
    volt = voltages.reshape(local_inputs, spec_local, frame)
    earlier = from_behind(volt[:, spec_local - history :, :], "tm", 1)
    weighted = filter_frames(jnp.concatenate([earlier, volt], axis=1), taps, spec_local)
    spectrum = transform(dft_table, weighted)
    flagged = (spectrum * flags.astype(jnp.float32).T[None, None]).astype(jnp.bfloat16)
    turned = lax.all_to_all(flagged, "chan", split_axis=0, concat_axis=3, tiled=True)
    rotation = offsets[0] * local_inputs
    scale = 1.0 / math.sqrt(spec_local * time_count)
    col_side = build_columns(turned[0, 0], turned[0, 1], rotation)
    row_side = jnp.concatenate([turned[0, 0], turned[0, 1]], axis=0)
    sums = lax.psum_scatter(products(row_side, col_side), "tm", scatter_dimension=0, tiled=True)
    return (sums * scale).astype(jnp.bfloat16)[None]


def solution(mesh):
    in_specs = (P("chan", "tm"), P(), P("chan", "tm"), P("chan"))
    out_specs = P("chan", "tm", None, None)
    return jax.shard_map(shards, mesh=mesh, in_specs=in_specs, out_specs=out_specs, check_vma=False)
```

profile of v0, /device:TPU:0, one launch (start us, length us, event | category | flops | bytes accessed | tf_op | source)
XLA Modules:
  0.0 958.3 jit_solution(2340111745106567445)
XLA Ops:
  6.5 0.0 copy-start.1
  6.5 0.0 copy-start
  6.5 44.7 %copy.47 = bf16[32,16,8,8192]{3,2,0,1:T(8,128)(2,1)} copy(bf16[32,16,8,8192]{3,2,1,0:T(8,128)(2,1)} %bitcast.26) | data formatting | bytes 134217728 | tf_op jit(solution)/shard_map/reshape | solution.py:67
  51.2 20.1 %slice.74 = bf16[256,7,8192]{2,0,1:T(8,128)(2,1)} slice(bf16[256,16,8192]{2,0,1:T(8,128)(2,1)} %bitcast.84), slice={[0:256], [9:16], [0:8192]} | slice | bytes 58720256 | tf_op jit(solution)/shard_map/slice | solution.py:68
  71.4 11.9 %collective-permute-start = (bf16[256,7,8192]{2,0,1:T(8,128)(2,1)}, bf16[256,7,8192]{2,0,1:T(8,128)(2,1)}, u32[]{:S(2)}, u32[]{:S(2)}) collective-permute-start(bf16[256,7,8192]{2,0,1:T(8,128)(2,1)} %slice.74), channel_id=1, source_target_pairs={{0,1},{1,2},{2,3},{4,5},{5,6},{6,7},{8,9},{9,10},{10,11},{12,13},{... | collective-permute-start | bytes 88080392 | tf_op jit(solution)/shard_map/ppermute | solution.py:14
  83.9 0.0 copy-done.1
  84.0 0.0 copy-done
  84.0 0.2 fusion.66
  84.2 1.1 cosine_multiply_fusion
  85.3 31.5 %collective-permute-done = bf16[256,7,8192]{2,0,1:T(8,128)(2,1)} collective-permute-done((bf16[256,7,8192]{2,0,1:T(8,128)(2,1)}, bf16[256,7,8192]{2,0,1:T(8,128)(2,1)}, u32[]{:S(2)}, u32[]{:S(2)}) %collective-permute-start) | collective-permute-done | bytes 29360160 | tf_op jit(solution)/shard_map/ppermute | solution.py:14
  116.8 20.1 %constant_dynamic-update-slice_fusion.1 = bf16[256,23,8192]{2,0,1:T(8,128)(2,1)} fusion(bf16[256,7,8192]{2,0,1:T(8,128)(2,1)} %collective-permute-done), kind=kLoop, calls=%fused_computation.79 | loop fusion | bytes 58720256
  136.9 44.7 %constant_dynamic-update-slice_fusion = bf16[256,23,8192]{2,0,1:T(8,128)(2,1)} fusion(bf16[256,23,8192]{2,0,1:T(8,128)(2,1)} %constant_dynamic-update-slice_fusion.1, bf16[32,16,8,8192]{3,2,1,0:T(8,128)(2,1)} %bitcast.26), kind=kLoop, calls=%fused_computation.78 | loop fusion | bytes 134217728 | tf_op jit(solution)/shard_map/concatenate | solution.py:69
  181.6 222.8 %fusion.47 = bf16[8,2,16,256]{3,0,1,2:T(8,128)(2,1)S(1)} fusion(bf16[256,23,8192]{2,0,1:T(8,128)(2,1)} %constant_dynamic-update-slice_fusion, f32[8192]{0:T(1024)S(1)} %bitcast.92, f32[8192]{0:T(1024)S(1)} %bitcast.93, f32[8192]{0:T(1024)S(1)} %bitcast.87, f32[8192]{0:T(1024)S(1)} %bitcast.88, f32[8192]{0:T(1024)S(1)} %bitcast.89, f32[8192]{0:T(1024)S(1)} %bitcast.90, ...), kind=kOutput, calls=%fused_computation.45 | convolution fusion | flops 7214465024 | bytes 537804800 | tf_op jit(solution)/shard_map/nkr,isn->krsi/dot_general | solution.py:40
  404.4 0.8 copy.22
  405.2 6.7 all-to-all-start
  411.8 0.2 reduce-scatter.2.cloned.1.call-start
  412.1 7.1 all-to-all-done
  419.2 0.1 copy.23
  419.3 0.1 all_to_all.16
  419.4 0.2 fusion.64
  419.6 13.2 %fusion.55 = f32[2048,2,2048]{2,0,1:T(8,128)} fusion(bf16[16,2048]{1,0:T(8,128)(2,1)S(1)} %get-tuple-element.16, bf16[16,2048]{1,0:T(8,128)(2,1)S(1)} %get-tuple-element.17, bf16[32,1,2048]{2,0,1:T(8,128)(2,1)S(1)} %get-tuple-element.19, bf16[32,1,2048]{2,0,1:T(8,128)(2,1)S(1)} %get-tuple-element.18), kind=kOutput, calls=%fused_computation.57 | convolution fusion | flops 537264128 | bytes 33947648 | tf_op jit(solution)/shard_map/dot_general | solution.py:54
  432.8 0.0 reduce-scatter.2.cloned.1.call-update
  432.9 507.7 %reduce-scatter.2.cloned.1.call-done = f32[512,2,2048]{2,0,1:T(8,128)} async-done(((f32[2048,2,2048]{2,0,1:T(8,128)}), f32[512,2,2048]{2,0,1:T(8,128)}) %reduce-scatter.2.cloned.1.call-update) | async-done | bytes 8388624 | tf_op jit(solution)/shard_map/reduce_scatter | solution.py:77
  940.6 4.5 fusion.40
  945.1 6.3 copy.26
  (5 shorter events, 0.0 us)
Async XLA Ops:
  6.5 77.4 %copy-start.1 = (s32[256,16]{0,1:T(8,128)S(1)}, s32[256,16]{0,1:T(8,128)}, u32[]{:S(2)}) copy-start(s32[256,16]{0,1:T(8,128)} %param.8) | copy-start | bytes 49156
  6.5 77.4 %copy-start = (f32[8,8192]{1,0:T(8,128)S(1)}, f32[8,8192]{1,0:T(8,128)}, u32[]{:S(2)}) copy-start(f32[8,8192]{1,0:T(8,128)} %param.7) | copy-start | bytes 786436
  71.4 45.5 %collective-permute-start = (bf16[256,7,8192]{2,0,1:T(8,128)(2,1)}, bf16[256,7,8192]{2,0,1:T(8,128)(2,1)}, u32[]{:S(2)}, u32[]{:S(2)}) collective-permute-start(bf16[256,7,8192]{2,0,1:T(8,128)(2,1)} %slice.74), channel_id=1, source_target_pairs={{0,1},{1,2},{2,3},{4,5},{5,6},{6,7},{8,9},{9,10},{10,11},{12,13},{... | collective-permute-start | bytes 88080392 | tf_op jit(solution)/shard_map/ppermute | solution.py:14
  405.2 14.0 %all-to-all-start = ((bf16[8,2,16,256]{3,1,2,0:T(2,128)(2,1)}), bf16[8,2,16,256]{3,1,2,0:T(2,128)(2,1)S(1)}, u32[]{:S(2)}, u32[]{:S(2)}) async-start(bf16[8,2,16,256]{3,1,2,0:T(2,128)(2,1)} %copy.22), calls=%async_computation | async-start | bytes 262144 | tf_op jit(solution)/shard_map/all_to_all | solution.py:72
  411.8 528.7 %reduce-scatter.2.cloned.1.call-start = ((), (), s32[]{:S(2)}) async-start(), calls=%async_computation.2 | async-start | bytes 41943040 | tf_op jit(solution)/shard_map/reduce_scatter | solution.py:77
Sparse Core Ops, SparseCore 0:
  433.0 507.5 reduce-scatter.1
where the time goes:
time: 959 us; the launch traced here: 958 us
  waiting for transfers between devices  546 us (57%)
  matrix products  236 us (25%)
  local copies, waits for them, and re-layouts  137 us (14%)
  starting transfers between devices  18.8 us (2%)
  between operations  14.2 us (1%)
    reduce_scatter x1, waiting for transfers between devices, shards(): lax.psum_scatter(products(row_side, col_side), 'tm', scatter_dimension=0,...  508 us
    dot_general x1, matrix products, transform(): jnp.einsum('nkr,isn->krsi', dft_table, weighted, precision=lax.Precision....  223 us
    concatenate x1, local copies, waits for them, and re-layouts, shards(): jnp.concatenate([earlier, volt], axis=1)  44.7 us
    reshape x1, local copies, waits for them, and re-layouts, shards(): volt = voltages.reshape(local_inputs, spec_local, frame)  44.7 us
    ppermute x1, waiting for transfers between devices, from_behind(): return lax.ppermute(block, axis, route)  31.5 us
    slice x1, local copies, waits for them, and re-layouts, shards(): earlier = from_behind(volt[:, spec_local - history:, :], 'tm', 1)  20.1 us
    unnamed x5, local copies, waits for them, and re-layouts  20.1 us
  transfers between devices with their start and end apart: 3, of which 3 were waited for; matrix products, arithmetic and copies ran while one was open for 0% of the time, Pallas kernels for 0%

commit v1 on v0

v1 whole, which is shorter than its diff:
```python
import functools
import math

import jax
import jax.numpy as jnp
from jax import lax
from jax.experimental import pallas as pl
from jax.experimental.pallas import tpu as pltpu
from jax.sharding import PartitionSpec as P

MIB = 1024 * 1024


def channel_table(frame, channels, width, shift):
    period = 4 * channels
    row = lax.broadcasted_iota(jnp.int32, (2 * channels, width), 0)
    sample = lax.broadcasted_iota(jnp.int32, (2 * channels, width), 1) + shift
    phase = (2 * (row // 2) + 1) * sample % period
    angle = phase.astype(jnp.float32) * (2.0 * math.pi / period)
    norm_scale = 1.0 / math.sqrt(frame)
    return jnp.where(row % 2 == 0, jnp.cos(angle), -jnp.sin(angle)) * norm_scale


def filterbank_kernel(spec, rows, taps, chunk, block, table, tap_ref, volt, own, tail, held, weights, total, sems):
    step, steps = pl.program_id(0), pl.num_programs(0)
    frame = steps * chunk
    pairs = table.shape[0]
    cols = taps * pairs

    def fetch(index, slot):
        for f in range(spec):
            pltpu.make_async_copy(
                volt.at[:, pl.ds(pl.multiple_of(f * frame + index * chunk, chunk), chunk)],
                held.at[slot, pl.ds(f * rows, rows), :],
                sems.at[slot, f],
            ).start()

    def arrive(slot):
        for f in range(spec):
            pltpu.make_async_copy(
                volt.at[:, pl.ds(0, chunk)], held.at[slot, pl.ds(f * rows, rows), :], sems.at[slot, f]
            ).wait()

    slot = lax.rem(step, 2)

    @pl.when(step == 0)
    def _():
        fetch(0, 0)
        total[...] = jnp.zeros_like(total)

    @pl.when(step + 1 < steps)
    def _():
        fetch(step + 1, 1 - slot)

    for t in range(taps):
        exact = tap_ref[t : t + 1, :] * table[...]
        high = exact.astype(jnp.bfloat16)
        low = (exact - high.astype(jnp.float32)).astype(jnp.bfloat16)
        weights[t * pairs : (t + 1) * pairs, :] = high
        weights[cols + t * pairs : cols + (t + 1) * pairs, :] = low

    arrive(slot)

    @pl.loop(0, spec * rows // block)
    def _(m):
        span = pl.ds(pl.multiple_of(m * block, block), block)
        total[span, :] += lax.dot_general(
            held[slot, span, :], weights[...], (((1,), (1,)), ((), ())), preferred_element_type=jnp.float32
        )

    @pl.when(step == steps - 1)
    def _():
        flipped = []
        for f in range(spec):
            part = total[f * rows : (f + 1) * rows, :]
            flipped.append((part[:, :cols] + part[:, cols:]).T)
        for f in range(spec + taps - 1):
            terms = [
                flipped[f - t][t * pairs : (t + 1) * pairs, :] for t in range(taps) if 0 <= f - t < spec
            ]
            value = functools.reduce(lambda a, b: a + b, terms)
            if f < spec:
                own[:, f, :] = value
            else:
                tail[:, f - spec, :] = value


def filterbank(volt, taps, table, spec, chunk, block):
    rows, width = volt.shape
    count, frame = taps.shape
    pairs = table.shape[0]
    cols = count * pairs
    return pl.pallas_call(
        functools.partial(filterbank_kernel, spec, rows, count, chunk, block),
        grid=(frame // chunk,),
        in_specs=[
            pl.BlockSpec((pairs, chunk), lambda s: (0, 0)),
            pl.BlockSpec((count, chunk), lambda s: (0, s)),
            pl.BlockSpec(memory_space=pl.ANY),
        ],
        out_specs=[
            pl.BlockSpec((pairs, spec, rows), lambda s: (0, 0, 0)),
            pl.BlockSpec((pairs, count - 1, rows), lambda s: (0, 0, 0)),
        ],
        out_shape=[
            jax.ShapeDtypeStruct((pairs, spec, rows), jnp.float32),
            jax.ShapeDtypeStruct((pairs, count - 1, rows), jnp.float32),
        ],
        scratch_shapes=[
            pltpu.VMEM((2, spec * rows, chunk), jnp.bfloat16),
            pltpu.VMEM((2 * cols, chunk), jnp.bfloat16),
            pltpu.VMEM((spec * rows, 2 * cols), jnp.float32),
            pltpu.SemaphoreType.DMA((2, spec)),
        ],
        compiler_params=pltpu.CompilerParams(vmem_limit_bytes=56 * MIB, dimension_semantics=("arbitrary",)),
        cost_estimate=pl.CostEstimate(
            flops=4 * spec * rows * frame * cols, bytes_accessed=2 * rows * width, transcendentals=0
        ),
    )(table, taps, volt)


def correlate_kernel(scale, place, real, imag, cols, out):
    left = (((0,), (0,)), ((), ()))
    for part, side in ((0, real), (1, imag)):
        value = lax.dot_general(side[...], cols[...], left, preferred_element_type=jnp.float32)
        out[:, part, :] = (value * scale).astype(jnp.bfloat16)


def correlate(row_side, swapped, columns, rotation, scale, block):
    depth, rows = row_side.shape
    width = columns.shape[1]
    blocks = width // block
    return pl.pallas_call(
        functools.partial(correlate_kernel, scale),
        grid_spec=pltpu.PrefetchScalarGridSpec(
            num_scalar_prefetch=1,
            grid=(blocks,),
            in_specs=[
                pl.BlockSpec((depth, rows), lambda j, place: (0, 0)),
                pl.BlockSpec((depth, rows), lambda j, place: (0, 0)),
                pl.BlockSpec((depth, block), lambda j, place: (0, lax.rem(j + place[0], blocks))),
            ],
            out_specs=pl.BlockSpec((rows, 2, block), lambda j, place: (0, 0, j)),
        ),
        out_shape=jax.ShapeDtypeStruct((rows, 2, width), jnp.bfloat16),
        compiler_params=pltpu.CompilerParams(vmem_limit_bytes=56 * MIB, dimension_semantics=("arbitrary",)),
    )(rotation, row_side, swapped, columns)


def shards(voltages, taps, flags, offsets):
    chan_count = lax.axis_size("chan")
    time_count = lax.axis_size("tm")
    local_inputs = voltages.shape[0]
    spec_local = flags.shape[1]
    frame = voltages.shape[1] // spec_local
    history = taps.shape[0] - 1
    chunk = 512
    table = channel_table(frame, chan_count, chunk, jnp.minimum(offsets[0], 0))
    block = min(spec_local * local_inputs, 1024)
    own, tail = filterbank(voltages, taps, table, spec_local, chunk, block)
    earlier = lax.ppermute(tail, "tm", [(i, i + 1) for i in range(time_count - 1)])
    spectrum = own + jnp.pad(earlier, ((0, 0), (0, spec_local - history), (0, 0)))
    flagged = (spectrum * flags.astype(jnp.float32).T[None]).astype(jnp.bfloat16)
    flagged = flagged.reshape(chan_count, 2, spec_local, local_inputs)
    turned = lax.all_to_all(flagged, "chan", split_axis=0, concat_axis=0, tiled=True)
    gathered = lax.all_gather(turned, "tm")
    columns = jnp.transpose(gathered, (0, 2, 3, 1, 4)).reshape(time_count, 2, spec_local, -1)
    inputs = columns.shape[-1]
    own_rows = inputs // time_count
    row_side = lax.dynamic_slice_in_dim(columns, lax.axis_index("tm") * own_rows, own_rows, axis=3)
    swapped = jnp.stack([row_side[:, 1], -row_side[:, 0]], axis=1)
    flat = (-1, own_rows)
    scale = 1.0 / math.sqrt(spec_local * time_count)
    width = local_inputs if local_inputs % 128 == 0 else 0
    rotation = offsets * 1
    columns = columns.reshape(-1, inputs)
    if not width:
        columns = jnp.roll(columns, -offsets[0] * local_inputs, axis=1)
        rotation = offsets * 0
        width = 256
    return correlate(row_side.reshape(flat), swapped.reshape(flat), columns, rotation, scale, width)[None]


def solution(mesh):
    in_specs = (P("chan", "tm"), P(), P("chan", "tm"), P("chan"))
    out_specs = P("chan", "tm", None, None)
    return jax.shard_map(shards, mesh=mesh, in_specs=in_specs, out_specs=out_specs, check_vma=False)
```

time: 959 us -> 80.7 us (0.08)
  waiting for transfers between devices: 546 us -> 8.5 us
  matrix products: 236 us -> 0 us
  local copies, waits for them, and re-layouts: 137 us -> 1.93 us
  Pallas kernels: 0 us -> 45.6 us
  between operations: 14.2 us -> 0.71 us
  blocking collectives: 0 us -> 10.8 us
  starting transfers between devices: 18.8 us -> 9.02 us
    reduce_scatter x1 -> x0, waiting for transfers between devices: 508 us -> none  [shards(): lax.psum_scatter(products(row_side, col_side), 'tm', scatter_dimension=0,...]
    dot_general x2 -> x0, matrix products: 236 us -> none  [the longest x1 223 us: transform(): jnp.einsum('nkr,isn->krsi', dft_table, weighted, precision=lax.Precision....]
    pallas_call x0 -> x2, Pallas kernels: none -> 45.6 us  [the longest x1 37.2 us: filterbank(): pl.pallas_call(functools.partial(filterbank_kernel, spec, rows, count, ch...]
    concatenate x1 -> x0, local copies, waits for them, and re-layouts: 44.7 us -> none  [shards(): jnp.concatenate([earlier, volt], axis=1)]
    reshape x1, local copies, waits for them, and re-layouts: 44.7 us -> 0.05 us  [shards(): jnp.transpose(gathered, (0, 2, 3, 1, 4))]
    ppermute x1, waiting for transfers between devices: 31.5 us -> 1.15 us  [shards(): lax.ppermute(tail, 'tm', [(i, i + 1) for i in range(time_count - 1)])]
    slice x2 -> x0, local copies, waits for them, and re-layouts: 20.3 us -> none  [the longest x1 20.1 us: shards(): earlier = from_behind(volt[:, spec_local - history:, :], 'tm', 1)]
    unnamed x5 -> x3, local copies, waits for them, and re-layouts: 20.1 us -> 0.92 us
  transfers between devices with their start and end apart: 3 -> 2, of which waited for: 3 -> 2; matrix products, arithmetic and copies ran while one was open for 0% -> 0% of each run, Pallas kernels for 0% -> 0%
where the time goes in v1:
time: 80.7 us; the launch traced here: 79.8 us
  Pallas kernels  45.6 us (57%)
  blocking collectives  10.8 us (13%)
  starting transfers between devices  9.02 us (11%)
  waiting for transfers between devices  8.5 us (11%)
  other arithmetic  3.18 us (4%)
  local copies, waits for them, and re-layouts  1.93 us (2%)
    pallas_call x1, Pallas kernels, filterbank(): pl.pallas_call(functools.partial(filterbank_kernel, spec, rows, count, ch...  37.2 us
    all_gather x1, blocking collectives, shards(): gathered = lax.all_gather(turned, 'tm')  10.8 us
    pallas_call x1, Pallas kernels, correlate(): pl.pallas_call(functools.partial(correlate_kernel, scale), grid_spec=pltp...  8.44 us
    all_to_all x1, waiting for transfers between devices, shards(): lax.all_to_all(flagged, 'chan', split_axis=0, concat_axis=0, tiled=True)  7.35 us
    all_to_all x1, starting transfers between devices, shards(): lax.all_to_all(flagged, 'chan', split_axis=0, concat_axis=0, tiled=True)  6.66 us
    ppermute x1, starting transfers between devices, shards(): lax.ppermute(tail, 'tm', [(i, i + 1) for i in range(time_count - 1)])  2.37 us
    convert_element_type x1, other arithmetic, shards(): (spectrum * flags.astype(jnp.float32).T[None]).astype(jnp.bfloat16)  1.63 us
  transfers between devices with their start and end apart: 2, of which 2 were waited for; matrix products, arithmetic and copies ran while one was open for 0% of the time, Pallas kernels for 0%

profile of v1, /device:TPU:0, one launch (start us, length us, event | category | flops | bytes accessed | tf_op | source)
XLA Modules:
  0.0 79.8 jit_solution(2614939655245139703)
XLA Ops:
  0.0 0.0 copy-start
  0.7 0.8 %select_multiply_fusion.table = f32[16,512]{1,0:T(8,128)} fusion(s32[512]{0:T(512)S(1)} %iota_add_fusion, s32[16]{0:T(128)S(1)} %get-tuple-element.13, s32[16]{0:T(128)S(1)} %get-tuple-element.15, s32[16]{0:T(128)S(1)} %get-tuple-element.14, s32[16]{0:T(128)S(1)} %get-tuple-element.16, pred[16]{0:T(512)(128)(4,1)S(1)} %get-tuple-element.11, ...), kind=kLoop, calls=%fused_computation.9 | loop fusion | flops 180224 | bytes 35104 | tf_op jit(solution)/shard_map/mul | solution.py:21
  1.5 37.2 %shard_map.46 = (f32[16,16,256]{2,1,0:T(8,128)}, f32[16,7,256]{2,1,0:T(8,128)}) custom-call(f32[16,512]{1,0:T(8,128)} %select_multiply_fusion.table, f32[8,8192]{1,0:T(8,128)} %tap_ref.1, bf16[256,131072]{1,0:T(8,128)(2,1)} %volt.1), custom_call_target="tpu_custom_call" | custom-call | flops 17179869184 | bytes 67108864 | tf_op jit(solution)/shard_map/pallas_call | solution.py:93
  38.7 2.4 %collective-permute-start = (f32[16,7,256]{2,1,0:T(8,128)}, f32[16,7,256]{2,1,0:T(8,128)S(1)}, u32[]{:S(2)}, u32[]{:S(2)}) collective-permute-start(f32[16,7,256]{2,1,0:T(8,128)} %get-tuple-element.8), channel_id=1, source_target_pairs={{0,1},{1,2},{2,3},{4,5},{5,6},{6,7},{8,9},{9,10},{10,11},{12,13},{... | collective-permute-start | bytes 344072 | tf_op jit(solution)/shard_map/ppermute | solution.py:161
  41.1 0.0 copy-done
  41.1 1.1 %collective-permute-done = f32[16,7,256]{2,1,0:T(8,128)S(1)} collective-permute-done((f32[16,7,256]{2,1,0:T(8,128)}, f32[16,7,256]{2,1,0:T(8,128)S(1)}, u32[]{:S(2)}, u32[]{:S(2)}) %collective-permute-start) | collective-permute-done | bytes 114720 | tf_op jit(solution)/shard_map/ppermute | solution.py:161
  42.3 1.6 %multiply_convert_fusion = bf16[16,16,256]{2,1,0:T(8,128)(2,1)} fusion(f32[16,16,256]{2,1,0:T(8,128)} %get-tuple-element.7, f32[16,7,256]{2,1,0:T(8,128)S(1)} %collective-permute-done, f32[16,256]{1,0:T(8,128)S(1)} %convert_bitcast_fusion), kind=kLoop, calls=%fused_computation | loop fusion | flops 196608 | bytes 524288 | tf_op jit(solution)/shard_map/convert_element_type | solution.py:163
  43.9 6.7 %all-to-all-start = ((bf16[8,2,16,256]{3,2,1,0:T(8,128)(2,1)}), bf16[8,2,16,256]{3,2,1,0:T(8,128)(2,1)S(1)}, u32[]{:S(2)}, u32[]{:S(2)}) async-start(bf16[8,2,16,256]{3,2,1,0:T(8,128)(2,1)} %bitcast.2), calls=%async_computation | async-start | bytes 262144 | tf_op jit(solution)/shard_map/all_to_all | solution.py:165
  50.6 7.4 %all-to-all-done = bf16[8,2,16,256]{3,2,1,0:T(8,128)(2,1)S(1)} async-done(((bf16[8,2,16,256]{3,2,1,0:T(8,128)(2,1)}), bf16[8,2,16,256]{3,2,1,0:T(8,128)(2,1)S(1)}, u32[]{:S(2)}, u32[]{:S(2)}) %all-to-all-start) | async-done | bytes 131104 | tf_op jit(solution)/shard_map/all_to_all | solution.py:165
  57.9 10.8 %all-gather = bf16[32,2,16,256]{3,2,1,0:T(8,128)(2,1)S(1)} all-gather(bf16[8,2,16,256]{3,2,1,0:T(8,128)(2,1)S(1)} %all-to-all-done), channel_id=2, replica_groups=mesh['chan'=8,'tm'=4] {'tm'}, dimensions={0}, use_global_device_ids=true | all-gather | bytes 655360 | tf_op jit(solution)/shard_map/all_gather | solution.py:166
  68.7 0.3 copy.8
  69.0 0.9 %copy.11 = bf16[16,8,8,256]{3,1,2,0:T(8,128)(2,1)} copy(bf16[16,8,8,256]{3,2,1,0:T(8,128)(2,1)S(1)} %bitcast.18) | data formatting | bytes 1048576
  69.9 0.7 constant_dynamic-slice_fusion.1
  70.6 0.7 pad_maximum_fusion
  71.3 8.4 %shard_map.47 = bf16[512,2,2048]{2,1,0:T(2,128)(2,1)} custom-call(s32[1]{0:T(128)S(6)} %copy.12.place, bf16[128,512]{1,0:T(8,128)(2,1)} %bitcast.21, bf16[128,512]{1,0:T(8,128)(2,1)} %bitcast.22, bf16[128,2048]{1,0:T(8,128)(2,1)} %bitcast.17), custom_call_target="tpu_custom_call" | custom-call | tf_op jit(solution)/shard_map/pallas_call | solution.py:133
  (7 shorter events, 0.1 us)
Async XLA Ops:
  0.0 41.1 %copy-start = (s32[256,16]{0,1:T(8,128)S(1)}, s32[256,16]{0,1:T(8,128)}, u32[]{:S(2)}) copy-start(s32[256,16]{0,1:T(8,128)} %param.6) | copy-start | bytes 49156
  38.7 3.5 %collective-permute-start = (f32[16,7,256]{2,1,0:T(8,128)}, f32[16,7,256]{2,1,0:T(8,128)S(1)}, u32[]{:S(2)}, u32[]{:S(2)}) collective-permute-start(f32[16,7,256]{2,1,0:T(8,128)} %get-tuple-element.8), channel_id=1, source_target_pairs={{0,1},{1,2},{2,3},{4,5},{5,6},{6,7},{8,9},{9,10},{10,11},{12,13},{... | collective-permute-start | bytes 344072 | tf_op jit(solution)/shard_map/ppermute | solution.py:161
  43.9 14.0 %all-to-all-start = ((bf16[8,2,16,256]{3,2,1,0:T(8,128)(2,1)}), bf16[8,2,16,256]{3,2,1,0:T(8,128)(2,1)S(1)}, u32[]{:S(2)}, u32[]{:S(2)}) async-start(bf16[8,2,16,256]{3,2,1,0:T(8,128)(2,1)} %bitcast.2), calls=%async_computation | async-start | bytes 262144 | tf_op jit(solution)/shard_map/all_to_all | solution.py:165

commit v2 on v1

--- a/solution.py
+++ b/solution.py
@@ -6,9 +6,14 @@
 from jax import lax
 from jax.experimental import pallas as pl
 from jax.experimental.pallas import tpu as pltpu
+from jax.sharding import Mesh
 from jax.sharding import PartitionSpec as P
 
 MIB = 1024 * 1024
+ACROSS = (((1,), (1,)), ((), ()))
+DOWN = (((0,), (0,)), ((), ()))
+RING = 3
+PIECES = 4
 
 
 def channel_table(frame, channels, width, shift):
@@ -21,7 +26,7 @@
     return jnp.where(row % 2 == 0, jnp.cos(angle), -jnp.sin(angle)) * norm_scale
 
 
-def filterbank_kernel(spec, rows, taps, chunk, block, table, tap_ref, volt, own, tail, held, weights, total, sems):
+def narrow_filterbank_kernel(spec, rows, taps, chunk, block, table, tap_ref, volt, own, tail, held, weights, total, sems):
     step, steps = pl.program_id(0), pl.num_programs(0)
     frame = steps * chunk
     pairs = table.shape[0]
@@ -85,13 +90,13 @@
                 tail[:, f - spec, :] = value
 
 
-def filterbank(volt, taps, table, spec, chunk, block):
+def narrow_filterbank(volt, taps, table, spec, chunk, block):
     rows, width = volt.shape
     count, frame = taps.shape
     pairs = table.shape[0]
     cols = count * pairs
     return pl.pallas_call(
-        functools.partial(filterbank_kernel, spec, rows, count, chunk, block),
+        functools.partial(narrow_filterbank_kernel, spec, rows, count, chunk, block),
         grid=(frame // chunk,),
         in_specs=[
             pl.BlockSpec((pairs, chunk), lambda s: (0, 0)),
@@ -119,69 +124,228 @@
     )(table, taps, volt)
 
 
-def correlate_kernel(scale, place, real, imag, cols, out):
-    left = (((0,), (0,)), ((), ()))
-    for part, side in ((0, real), (1, imag)):
-        value = lax.dot_general(side[...], cols[...], left, preferred_element_type=jnp.float32)
+def filterbank_kernel(spec, rows, offset, tap_hbm, volt, own, tail, tap_ref, held, weights, folded, sems, tap_sem):
+    taps, frame = tap_ref.shape
+    pairs = own.shape[0]
+    cols = taps * pairs
+    width = frame // PIECES
+    pair_steps = (spec - 2) // 2
+
+    def piece(step, part, count, first):
+        slot = lax.rem(jnp.int32(step), RING)
+        copies = []
+        for n in range(count):
+            start = pl.multiple_of((first + n) * frame + part * width, width)
+            copies.append(
+                pltpu.make_async_copy(
+                    volt.at[:, pl.ds(start, width)],
+                    held.at[slot, pl.ds(n * rows, rows), pl.ds(part * width, width)],
+                    sems.at[slot, part],
+                )
+            )
+        return copies
+
+    def fetch_single(step, first):
+        for part in range(PIECES):
+            piece(step, part, 1, first)[0].start()
+
+    def fetch_pair(step):
+        slot = lax.rem(jnp.int32(step), RING)
+        for n in range(2):
+            start = pl.multiple_of((2 * step - 1 + n) * frame, frame)
+            pltpu.make_async_copy(
+                volt.at[:, pl.ds(start, frame)], held.at[slot, pl.ds(n * rows, rows), :], sems.at[slot, 0]
+            ).start()
+
+    def add(value, first, count):
+        value = value[:cols] + value[cols:]
+        for t in range(taps):
+            span = pl.ds(pl.multiple_of((first + t) * rows, rows), count * rows)
+            folded[:, span] += value[t * pairs : (t + 1) * pairs, :]
+
+    def single(step, first, prepare):
+        total = None
+        slot = step % RING
+        for part in range(PIECES):
+            prepare(part)
+            piece(step, part, 1, first)[0].wait()
+            span = slice(part * width, (part + 1) * width)
+            value = lax.dot_general(
+                weights[:, span], held[slot, :rows, span], ACROSS, preferred_element_type=jnp.float32
+            )
+            total = value if total is None else total + value
+        add(total, first, 1)
+
+    taps_copy = pltpu.make_async_copy(tap_hbm, tap_ref, tap_sem)
+    taps_copy.start()
+    fetch_single(0, 0)
+    fetch_pair(1)
+    folded[...] = jnp.zeros_like(folded)
+    table = channel_table(frame, pairs // 2, 128, jnp.minimum(offset[0], 0))
+    table = jnp.concatenate([table] * (width // 128), axis=1)
+    taps_copy.wait()
+
+    def build(part):
+        span = slice(part * width, (part + 1) * width)
+        for t in range(taps):
+            exact = tap_ref[t : t + 1, span] * table
+            high = exact.astype(jnp.bfloat16)
+            low = (exact - high.astype(jnp.float32)).astype(jnp.bfloat16)
+            weights[t * pairs : (t + 1) * pairs, span] = high
+            weights[cols + t * pairs : cols + (t + 1) * pairs, span] = low
+
+    fetch_pair(2)
+    single(0, 0, build)
+
+    @pl.loop(1, pair_steps + 1)
+    def _(step):
+        @pl.when(step + 2 <= pair_steps)
+        def _():
+            fetch_pair(step + 2)
+
+        @pl.when(step + 2 == pair_steps + 1)
+        def _():
+            fetch_single(pair_steps + 1, spec - 1)
+
+        slot = lax.rem(step, RING)
+        block = held.at[slot]
+        pltpu.make_async_copy(block, block, sems.at[slot, 0]).wait()
+        value = lax.dot_general(weights[...], block[...], ACROSS, preferred_element_type=jnp.float32)
+        add(value, 2 * step - 1, 2)
+
+    single(pair_steps + 1, spec - 1, lambda part: None)
+    for f in range(spec + taps - 1):
+        value = folded[:, f * rows : (f + 1) * rows]
+        if f < spec:
+            own[:, f, :] = value
+        else:
+            tail[:, f - spec, :] = value
+
+
+def filterbank(volt, taps, offsets, channels, spec):
+    rows, width = volt.shape
+    count, frame = taps.shape
+    pairs = 2 * channels
+    cols = count * pairs
+    return pl.pallas_call(
+        functools.partial(filterbank_kernel, spec, rows),
+        in_specs=[
+            pl.BlockSpec(memory_space=pltpu.SMEM),
+            pl.BlockSpec(memory_space=pl.ANY),
+            pl.BlockSpec(memory_space=pl.ANY),
+        ],
+        out_shape=[
+            jax.ShapeDtypeStruct((pairs, spec, rows), jnp.float32),
+            jax.ShapeDtypeStruct((pairs, count - 1, rows), jnp.float32),
+        ],
+        scratch_shapes=[
+            pltpu.VMEM((count, frame), jnp.float32),
+            pltpu.VMEM((RING, 2 * rows, frame), jnp.bfloat16),
+            pltpu.VMEM((2 * cols, frame), jnp.bfloat16),
+            pltpu.VMEM((pairs, (spec + count - 1) * rows), jnp.float32),
+            pltpu.SemaphoreType.DMA((RING, PIECES)),
+            pltpu.SemaphoreType.DMA,
+        ],
+        compiler_params=pltpu.CompilerParams(vmem_limit_bytes=56 * MIB),
+        cost_estimate=pl.CostEstimate(
+            flops=4 * spec * rows * frame * cols, bytes_accessed=2 * rows * width, transcendentals=0
+        ),
+    )(offsets, taps, volt)
+
+
+def correlate_kernel(scale, place, mine_rows, other_rows, mine_cols, other_cols, out, side):
+    blocks, wide, _, spec, lanes = mine_cols.shape
+    depth = 2 * wide * 2 * spec
+
+    @pl.when(pl.program_id(0) == 0)
+    def _():
+        for j in range(blocks):
+            turned = lax.rem(j + place[0], blocks)
+            at = 0
+            for source in (mine_cols, other_cols):
+                for x in range(wide):
+                    for part in range(2):
+                        side[at : at + spec, j * lanes : (j + 1) * lanes] = source[turned, x, part]
+                        at += spec
+
+    real, imag = [], []
+    for source in (mine_rows, other_rows):
+        for x in range(wide):
+            first, second = source[0, x, 0], source[0, x, 1]
+            real += [first, second]
+            imag += [second, -first]
+    for part, rows in ((0, real), (1, imag)):
+        value = lax.dot_general(
+            jnp.concatenate(rows, axis=0), side[...], DOWN, preferred_element_type=jnp.float32
+        )
         out[:, part, :] = (value * scale).astype(jnp.bfloat16)
 
 
-def correlate(row_side, swapped, columns, rotation, scale, block):
-    depth, rows = row_side.shape
-    width = columns.shape[1]
-    blocks = width // block
+def correlate(mine_rows, other_rows, mine_cols, other_cols, rotation, place, scale, own_rows):
+    blocks, wide, parts, spec, lanes = mine_cols.shape
+    own_blocks = own_rows // lanes
+    row_spec = pl.BlockSpec((1, wide, parts, spec, lanes), lambda i, place: (place[1] * own_blocks + i, 0, 0, 0, 0))
+    col_spec = pl.BlockSpec((blocks, wide, parts, spec, lanes), lambda i, place: (0, 0, 0, 0, 0))
     return pl.pallas_call(
         functools.partial(correlate_kernel, scale),
         grid_spec=pltpu.PrefetchScalarGridSpec(
             num_scalar_prefetch=1,
-            grid=(blocks,),
-            in_specs=[
-                pl.BlockSpec((depth, rows), lambda j, place: (0, 0)),
-                pl.BlockSpec((depth, rows), lambda j, place: (0, 0)),
-                pl.BlockSpec((depth, block), lambda j, place: (0, lax.rem(j + place[0], blocks))),
-            ],
-            out_specs=pl.BlockSpec((rows, 2, block), lambda j, place: (0, 0, j)),
+            grid=(own_blocks,),
+            in_specs=[row_spec, row_spec, col_spec, col_spec],
+            out_specs=pl.BlockSpec((lanes, 2, blocks * lanes), lambda i, place: (i, 0, 0)),
+            scratch_shapes=[pltpu.VMEM((2 * wide * 2 * spec, blocks * lanes), jnp.bfloat16)],
         ),
-        out_shape=jax.ShapeDtypeStruct((rows, 2, width), jnp.bfloat16),
+        out_shape=jax.ShapeDtypeStruct((own_rows, 2, blocks * lanes), jnp.bfloat16),
         compiler_params=pltpu.CompilerParams(vmem_limit_bytes=56 * MIB, dimension_semantics=("arbitrary",)),
-    )(rotation, row_side, swapped, columns)
+    )(jnp.stack([rotation, place]), mine_rows, other_rows, mine_cols, other_cols)
+
+
+def regroup(pieces, lanes):
+    blocks, wide, parts, spec, narrow = pieces.shape
+    join = lanes // narrow
+    pieces = pieces.reshape(blocks // join, join, wide, parts, spec, narrow)
+    return jnp.transpose(pieces, (0, 2, 3, 4, 1, 5)).reshape(blocks // join, wide, parts, spec, lanes)
 
 
 def shards(voltages, taps, flags, offsets):
-    chan_count = lax.axis_size("chan")
-    time_count = lax.axis_size("tm")
+    chan_count, wide, cores = (lax.axis_size(name) for name in ("chan", "wide", "core"))
+    time_count = wide * cores
     local_inputs = voltages.shape[0]
+    inputs = local_inputs * chan_count
     spec_local = flags.shape[1]
     frame = voltages.shape[1] // spec_local
     history = taps.shape[0] - 1
-    chunk = 512
-    table = channel_table(frame, chan_count, chunk, jnp.minimum(offsets[0], 0))
-    block = min(spec_local * local_inputs, 1024)
-    own, tail = filterbank(voltages, taps, table, spec_local, chunk, block)
-    earlier = lax.ppermute(tail, "tm", [(i, i + 1) for i in range(time_count - 1)])
+    aligned = local_inputs % 128 == 0 and 128 % (4 * chan_count) == 0
+    if aligned:
+        own, tail = filterbank(voltages, taps, offsets, chan_count, spec_local)
+    else:
+        table = channel_table(frame, chan_count, 512, jnp.minimum(offsets[0], 0))
+        own, tail = narrow_filterbank(voltages, taps, table, spec_local, 512, spec_local * local_inputs)
+    earlier = lax.ppermute(tail, ("wide", "core"), [(i, i + 1) for i in range(time_count - 1)])
     spectrum = own + jnp.pad(earlier, ((0, 0), (0, spec_local - history), (0, 0)))
     flagged = (spectrum * flags.astype(jnp.float32).T[None]).astype(jnp.bfloat16)
-    flagged = flagged.reshape(chan_count, 2, spec_local, local_inputs)
-    turned = lax.all_to_all(flagged, "chan", split_axis=0, concat_axis=0, tiled=True)
-    gathered = lax.all_gather(turned, "tm")
-    columns = jnp.transpose(gathered, (0, 2, 3, 1, 4)).reshape(time_count, 2, spec_local, -1)
-    inputs = columns.shape[-1]
+    flagged = flagged.reshape(chan_count, 1, 2, spec_local, local_inputs)
+    sent = jnp.broadcast_to(flagged, (chan_count, wide, 2, spec_local, local_inputs))
+    sent = sent.reshape(chan_count * wide, 2, spec_local, local_inputs)
+    mine = lax.all_to_all(sent, ("chan", "wide"), split_axis=0, concat_axis=0, tiled=True)
+    other = lax.ppermute(mine, "core", [(0, 1), (1, 0)])
+    shape = (chan_count, wide, 2, spec_local, local_inputs)
+    mine, other = mine.reshape(shape), other.reshape(shape)
+    scale = 1.0 / math.sqrt(spec_local * time_count)
     own_rows = inputs // time_count
-    row_side = lax.dynamic_slice_in_dim(columns, lax.axis_index("tm") * own_rows, own_rows, axis=3)
-    swapped = jnp.stack([row_side[:, 1], -row_side[:, 0]], axis=1)
-    flat = (-1, own_rows)
-    scale = 1.0 / math.sqrt(spec_local * time_count)
-    width = local_inputs if local_inputs % 128 == 0 else 0
-    rotation = offsets * 1
-    columns = columns.reshape(-1, inputs)
-    if not width:
-        columns = jnp.roll(columns, -offsets[0] * local_inputs, axis=1)
-        rotation = offsets * 0
-        width = 256
-    return correlate(row_side.reshape(flat), swapped.reshape(flat), columns, rotation, scale, width)[None]
+    place = lax.axis_index(("wide", "core"))
+    if aligned:
+        return correlate(mine, other, mine, other, offsets[0], place, scale, own_rows)[None]
+    lanes = 256
+    rows = [regroup(pieces, lanes) for pieces in (mine, other)]
+    cols = [regroup(jnp.roll(pieces, -offsets[0], axis=0), lanes) for pieces in (mine, other)]
+    return correlate(*rows, *cols, offsets[0] * 0, place, scale, own_rows)[None]
 
 
 def solution(mesh):
-    in_specs = (P("chan", "tm"), P(), P("chan", "tm"), P("chan"))
-    out_specs = P("chan", "tm", None, None)
-    return jax.shard_map(shards, mesh=mesh, in_specs=in_specs, out_specs=out_specs, check_vma=False)
+    devices = mesh.devices.reshape(mesh.shape["chan"], -1, 2)
+    split = Mesh(devices, ("chan", "wide", "core"))
+    time = ("wide", "core")
+    in_specs = (P("chan", time), P(), P("chan", time), P("chan"))
+    out_specs = P("chan", time, None, None)
+    return jax.shard_map(shards, mesh=split, in_specs=in_specs, out_specs=out_specs, check_vma=False)

time: 80.7 us -> 60.2 us (0.75)
  Pallas kernels: 45.6 us -> 32.9 us
  blocking collectives: 10.8 us -> 19.6 us
  starting transfers between devices: 9.02 us -> 2.37 us
  waiting for transfers between devices: 8.5 us -> 2.01 us
  other arithmetic: 3.18 us -> 1.65 us
  local copies, waits for them, and re-layouts: 1.93 us -> 0.72 us
    all_to_all x0 -> x1, blocking collectives: none -> 19.6 us  [shards(): lax.all_to_all(sent, ('chan', 'wide'), split_axis=0, concat_axis=0, tiled...]
    all_gather x1 -> x0, blocking collectives: 10.8 us -> none  [shards(): gathered = lax.all_gather(turned, 'tm')]
    pallas_call x1, Pallas kernels: 37.2 us -> 27.4 us  [filterbank(): pl.pallas_call(functools.partial(filterbank_kernel, spec, rows), in_specs...]
    all_to_all x1 -> x0, waiting for transfers between devices: 7.35 us -> none  [shards(): lax.all_to_all(flagged, 'chan', split_axis=0, concat_axis=0, tiled=True)]
    all_to_all x1 -> x0, starting transfers between devices: 6.66 us -> none  [shards(): lax.all_to_all(flagged, 'chan', split_axis=0, concat_axis=0, tiled=True)]
    pallas_call x1, Pallas kernels: 8.44 us -> 5.53 us  [correlate(): pl.pallas_call(functools.partial(correlate_kernel, scale), grid_spec=pltp...]
    ppermute x1 -> x2, waiting for transfers between devices: 1.15 us -> 2.01 us  [the longest x1 1.15 us: shards(): lax.ppermute(tail, ('wide', 'core'), [(i, i + 1) for i in range(time_coun...]
    mul x1 -> x0, other arithmetic: 0.83 us -> none  [channel_table(): return jnp.where(row % 2 == 0, jnp.cos(angle), -jnp.sin(angle)) * norm_scale]
  transfers between devices with their start and end apart: 2 -> 2, of which waited for: 2 -> 2; matrix products, arithmetic and copies ran while one was open for 0% -> 1% of each run, Pallas kernels for 0% -> 0%
where the time goes in v2:
time: 60.2 us; the launch traced here: 59.9 us
  Pallas kernels  32.9 us (55%)
  blocking collectives  19.6 us (33%)
  starting transfers between devices  2.37 us (4%)
  waiting for transfers between devices  2.01 us (3%)
  other arithmetic  1.65 us (3%)
  local copies, waits for them, and re-layouts  0.72 us (1%)
  between operations  0.71 us (1%)
    pallas_call x1, Pallas kernels, filterbank(): pl.pallas_call(functools.partial(filterbank_kernel, spec, rows), in_specs...  27.4 us
    all_to_all x1, blocking collectives, shards(): lax.all_to_all(sent, ('chan', 'wide'), split_axis=0, concat_axis=0, tiled...  19.6 us
    pallas_call x1, Pallas kernels, correlate(): pl.pallas_call(functools.partial(correlate_kernel, scale), grid_spec=pltp...  5.53 us
    ppermute x1, starting transfers between devices, shards(): lax.ppermute(tail, ('wide', 'core'), [(i, i + 1) for i in range(time_coun...  2.37 us
  transfers between devices with their start and end apart: 2, of which 2 were waited for; matrix products, arithmetic and copies ran while one was open for 1% of the time, Pallas kernels for 0%

profile of v2, /device:TPU:0, one launch (start us, length us, event | category | flops | bytes accessed | tf_op | source)
XLA Modules:
  0.0 59.9 jit_solution(2247753195621776383)
XLA Ops:
  0.0 0.0 copy-start.2
  0.7 27.4 %shard_map.46 = (f32[16,16,256]{2,1,0:T(8,128)}, f32[16,7,256]{2,1,0:T(8,128)}) custom-call(s32[1]{0:T(128)S(6)} %copy.5.offset, f32[8,8192]{1,0:T(8,128)} %tap_hbm.1, bf16[256,131072]{1,0:T(8,128)(2,1)} %volt.1), custom_call_target="tpu_custom_call" | custom-call | flops 17179869184 | bytes 67108864 | tf_op jit(solution)/shard_map/pallas_call | solution.py:230
  28.1 2.4 %collective-permute-start = (f32[16,7,256]{2,1,0:T(8,128)}, f32[16,7,256]{2,1,0:T(8,128)S(1)}, u32[]{:S(2)}, u32[]{:S(2)}) collective-permute-start(f32[16,7,256]{2,1,0:T(8,128)} %get-tuple-element.8), channel_id=1, source_target_pairs={{0,1},{1,2},{2,3},{4,5},{5,6},{6,7},{8,9},{9,10},{10,11},{12,13},{... | collective-permute-start | bytes 344072 | tf_op jit(solution)/shard_map/ppermute | solution.py:324
  30.4 0.0 copy-done.2
  30.4 1.1 %collective-permute-done = f32[16,7,256]{2,1,0:T(8,128)S(1)} collective-permute-done((f32[16,7,256]{2,1,0:T(8,128)}, f32[16,7,256]{2,1,0:T(8,128)S(1)}, u32[]{:S(2)}, u32[]{:S(2)}) %collective-permute-start) | collective-permute-done | bytes 114720 | tf_op jit(solution)/shard_map/ppermute | solution.py:324
  31.6 1.0 %multiply_convert_fusion = bf16[16,16,256]{2,1,0:T(8,128)(2,1)S(1)} fusion(f32[16,16,256]{2,1,0:T(8,128)} %get-tuple-element.7, f32[16,7,256]{2,1,0:T(8,128)S(1)} %collective-permute-done, f32[16,256]{1,0:T(8,128)S(1)} %convert_bitcast_fusion), kind=kLoop, calls=%fused_computation | loop fusion | flops 196608 | bytes 524288 | tf_op jit(solution)/shard_map/convert_element_type | solution.py:326
  32.6 19.6 %all_to_all.5 = bf16[16,2,16,256]{3,2,1,0:T(8,128)(2,1)S(1)} all-to-all(bf16[16,2,16,256]{3,2,1,0:T(8,128)(2,1)S(1)} %bitcast.10), channel_id=1, replica_groups=mesh['chan'=8,'wide'=2,'core'=2] {'chan','wide'}, dimensions={0} | all-to-all | bytes 524288 | tf_op jit(solution)/shard_map/all_to_all | solution.py:330
  52.2 0.0 copy-start
  52.2 0.0 collective-permute-start.1
  52.2 0.7 %pad_add_fusion.place = s32[2]{0:T(128)} fusion(s32[1]{0:T(128)} %bitcast, s32[1]{0:T(128)S(6)} %copy.5.offset), kind=kLoop, calls=%fused_computation.2 | loop fusion | flops 2 | bytes 16 | tf_op jit(solution)/shard_map/stack | solution.py:300
  52.9 0.9 %collective-permute-done.1 = bf16[16,2,16,256]{3,2,1,0:T(8,128)(2,1)S(1)} collective-permute-done((bf16[16,2,16,256]{3,2,1,0:T(8,128)(2,1)S(1)}, bf16[16,2,16,256]{3,2,1,0:T(8,128)(2,1)S(1)}, u32[]{:S(2)}, u32[]{:S(2)}) %collective-permute-start.1) | collective-permute-done | bytes 262176 | tf_op jit(solution)/shard_map/ppermute | solution.py:331
  53.7 0.0 copy-start.1
  53.7 0.0 copy-done
  53.7 0.7 %copy-done.1 = bf16[16,2,16,256]{3,2,1,0:T(8,128)(2,1)} copy-done((bf16[16,2,16,256]{3,2,1,0:T(8,128)(2,1)}, bf16[16,2,16,256]{3,2,1,0:T(8,128)(2,1)S(1)}, u32[]{:S(2)}) %copy-start.1) | copy-done | bytes 262168
  54.4 5.5 %shard_map.47 = bf16[512,2,2048]{2,1,0:T(2,128)(2,1)} custom-call(s32[2]{0:T(128)} %pad_add_fusion.place, bf16[8,2,2,16,256]{4,3,2,1,0:T(8,128)(2,1)} %bitcast.8, bf16[8,2,2,16,256]{4,3,2,1,0:T(8,128)(2,1)} %bitcast.11, bf16[8,2,2,16,256]{4,3,2,1,0:T(8,128)(2,1)} %bitcast.9, bf16[8,2,2,16,256]{4,3,2,1,0:T(8,128)(2,1)} %bitcast.12), custom_call_target="tpu_custom_call" | custom-call | tf_op jit(solution)/shard_map/pallas_call | solution.py:289
  (2 shorter events, 0.0 us)
Async XLA Ops:
  0.0 30.4 %copy-start.2 = (s32[256,16]{0,1:T(8,128)S(1)}, s32[256,16]{0,1:T(8,128)}, u32[]{:S(2)}) copy-start(s32[256,16]{0,1:T(8,128)} %param.6) | copy-start | bytes 49156
  28.1 3.5 %collective-permute-start = (f32[16,7,256]{2,1,0:T(8,128)}, f32[16,7,256]{2,1,0:T(8,128)S(1)}, u32[]{:S(2)}, u32[]{:S(2)}) collective-permute-start(f32[16,7,256]{2,1,0:T(8,128)} %get-tuple-element.8), channel_id=1, source_target_pairs={{0,1},{1,2},{2,3},{4,5},{5,6},{6,7},{8,9},{9,10},{10,11},{12,13},{... | collective-permute-start | bytes 344072 | tf_op jit(solution)/shard_map/ppermute | solution.py:324
  52.2 1.5 %copy-start = (bf16[16,2,16,256]{3,2,1,0:T(8,128)(2,1)}, bf16[16,2,16,256]{3,2,1,0:T(8,128)(2,1)S(1)}, u32[]{:S(2)}) copy-start(bf16[16,2,16,256]{3,2,1,0:T(8,128)(2,1)S(1)} %all_to_all.5) | copy-start | bytes 786436
  52.2 1.5 %collective-permute-start.1 = (bf16[16,2,16,256]{3,2,1,0:T(8,128)(2,1)S(1)}, bf16[16,2,16,256]{3,2,1,0:T(8,128)(2,1)S(1)}, u32[]{:S(2)}, u32[]{:S(2)}) collective-permute-start(bf16[16,2,16,256]{3,2,1,0:T(8,128)(2,1)S(1)} %all_to_all.5), channel_id=1, source_target_pairs={{0,1},{1,0},{2,3},{3,2},{4,5},{5,4},{6,7},{7,6},{8,9},{9,8},{10,11... | collective-permute-start | bytes 786440 | tf_op jit(solution)/shard_map/ppermute | solution.py:331
  53.7 0.7 %copy-start.1 = (bf16[16,2,16,256]{3,2,1,0:T(8,128)(2,1)}, bf16[16,2,16,256]{3,2,1,0:T(8,128)(2,1)S(1)}, u32[]{:S(2)}) copy-start(bf16[16,2,16,256]{3,2,1,0:T(8,128)(2,1)S(1)} %collective-permute-done.1) | copy-start | bytes 786436

commit v3 on v2

--- a/solution.py
+++ b/solution.py
@@ -12,8 +12,8 @@
 MIB = 1024 * 1024
 ACROSS = (((1,), (1,)), ((), ()))
 DOWN = (((0,), (0,)), ((), ()))
-RING = 3
-PIECES = 4
+GROUP = 1
+AHEAD = 3
 
 
 def channel_table(frame, channels, width, shift):
@@ -128,65 +128,38 @@
     taps, frame = tap_ref.shape
     pairs = own.shape[0]
     cols = taps * pairs
-    width = frame // PIECES
-    pair_steps = (spec - 2) // 2
-
-    def piece(step, part, count, first):
-        slot = lax.rem(jnp.int32(step), RING)
-        copies = []
-        for n in range(count):
-            start = pl.multiple_of((first + n) * frame + part * width, width)
-            copies.append(
+    ring = held.shape[0]
+    steps = spec // GROUP
+    strip = 512
+
+    def copies(step):
+        slot = lax.rem(step, ring)
+        made = []
+        for n in range(GROUP):
+            start = pl.multiple_of((step * GROUP + n) * frame, frame)
+            made.append(
                 pltpu.make_async_copy(
-                    volt.at[:, pl.ds(start, width)],
-                    held.at[slot, pl.ds(n * rows, rows), pl.ds(part * width, width)],
-                    sems.at[slot, part],
+                    volt.at[:, pl.ds(start, frame)], held.at[slot, pl.ds(n * rows, rows), :], sems.at[slot]
                 )
             )
-        return copies
-
-    def fetch_single(step, first):
-        for part in range(PIECES):
-            piece(step, part, 1, first)[0].start()
-
-    def fetch_pair(step):
-        slot = lax.rem(jnp.int32(step), RING)
-        for n in range(2):
-            start = pl.multiple_of((2 * step - 1 + n) * frame, frame)
-            pltpu.make_async_copy(
-                volt.at[:, pl.ds(start, frame)], held.at[slot, pl.ds(n * rows, rows), :], sems.at[slot, 0]
-            ).start()
-
-    def add(value, first, count):
-        value = value[:cols] + value[cols:]
-        for t in range(taps):
-            span = pl.ds(pl.multiple_of((first + t) * rows, rows), count * rows)
-            folded[:, span] += value[t * pairs : (t + 1) * pairs, :]
-
-    def single(step, first, prepare):
-        total = None
-        slot = step % RING
-        for part in range(PIECES):
-            prepare(part)
-            piece(step, part, 1, first)[0].wait()
-            span = slice(part * width, (part + 1) * width)
-            value = lax.dot_general(
-                weights[:, span], held[slot, :rows, span], ACROSS, preferred_element_type=jnp.float32
-            )
-            total = value if total is None else total + value
-        add(total, first, 1)
+        return made
 
     taps_copy = pltpu.make_async_copy(tap_hbm, tap_ref, tap_sem)
     taps_copy.start()
-    fetch_single(0, 0)
-    fetch_pair(1)
+
+    @pl.loop(0, AHEAD)
+    def _(step):
+        for copy in copies(step):
+            copy.start()
+
     folded[...] = jnp.zeros_like(folded)
     table = channel_table(frame, pairs // 2, 128, jnp.minimum(offset[0], 0))
-    table = jnp.concatenate([table] * (width // 128), axis=1)
+    table = jnp.concatenate([table] * (strip // 128), axis=1)
     taps_copy.wait()
 
-    def build(part):
-        span = slice(part * width, (part + 1) * width)
+    @pl.loop(0, frame // strip)
+    def _(s):
+        span = pl.ds(pl.multiple_of(s * strip, strip), strip)
         for t in range(taps):
             exact = tap_ref[t : t + 1, span] * table
             high = exact.astype(jnp.bfloat16)
@@ -194,26 +167,23 @@
             weights[t * pairs : (t + 1) * pairs, span] = high
             weights[cols + t * pairs : cols + (t + 1) * pairs, span] = low
 
-    fetch_pair(2)
-    single(0, 0, build)
-
-    @pl.loop(1, pair_steps + 1)
+    @pl.loop(0, steps)
     def _(step):
-        @pl.when(step + 2 <= pair_steps)
+        slot = lax.rem(step, ring)
+        block = held.at[slot]
+        pltpu.make_async_copy(block, block, sems.at[slot]).wait()
+
+        @pl.when(step + AHEAD < steps)
         def _():
-            fetch_pair(step + 2)
-
-        @pl.when(step + 2 == pair_steps + 1)
-        def _():
-            fetch_single(pair_steps + 1, spec - 1)
-
-        slot = lax.rem(step, RING)
-        block = held.at[slot]
-        pltpu.make_async_copy(block, block, sems.at[slot, 0]).wait()
+            for copy in copies(step + AHEAD):
+                copy.start()
+
         value = lax.dot_general(weights[...], block[...], ACROSS, preferred_element_type=jnp.float32)
-        add(value, 2 * step - 1, 2)
-
-    single(pair_steps + 1, spec - 1, lambda part: None)
+        value = value[:cols] + value[cols:]
+        for t in range(taps):
+            span = pl.ds(pl.multiple_of((step * GROUP + t) * rows, rows), GROUP * rows)
+            folded[:, span] += value[t * pairs : (t + 1) * pairs, :]
+
     for f in range(spec + taps - 1):
         value = folded[:, f * rows : (f + 1) * rows]
         if f < spec:
@@ -240,10 +210,10 @@
         ],
         scratch_shapes=[
             pltpu.VMEM((count, frame), jnp.float32),
-            pltpu.VMEM((RING, 2 * rows, frame), jnp.bfloat16),
+            pltpu.VMEM((AHEAD + 1, GROUP * rows, frame), jnp.bfloat16),
             pltpu.VMEM((2 * cols, frame), jnp.bfloat16),
             pltpu.VMEM((pairs, (spec + count - 1) * rows), jnp.float32),
-            pltpu.SemaphoreType.DMA((RING, PIECES)),
+            pltpu.SemaphoreType.DMA((AHEAD + 1,)),
             pltpu.SemaphoreType.DMA,
         ],
         compiler_params=pltpu.CompilerParams(vmem_limit_bytes=56 * MIB),
@@ -253,51 +223,62 @@
     )(offsets, taps, volt)
 
 
-def correlate_kernel(scale, place, mine_rows, other_rows, mine_cols, other_cols, out, side):
-    blocks, wide, _, spec, lanes = mine_cols.shape
-    depth = 2 * wide * 2 * spec
-
-    @pl.when(pl.program_id(0) == 0)
+def correlate_kernel(scale, rotation, *refs):
+    sources, (out, side, weave) = refs[:-3], refs[-3:]
+    rows, columns = sources[:2], sources[-2:]
+    blocks, wide, _, spec, lanes = columns[0].shape
+    step = pl.program_id(0)
+
+    @pl.when(step == 0)
     def _():
         for j in range(blocks):
-            turned = lax.rem(j + place[0], blocks)
+            turned = lax.rem(j + rotation[0], blocks)
             at = 0
-            for source in (mine_cols, other_cols):
+            for source in columns:
                 for x in range(wide):
                     for part in range(2):
                         side[at : at + spec, j * lanes : (j + 1) * lanes] = source[turned, x, part]
                         at += spec
-
+        taken = lax.broadcasted_iota(jnp.int32, weave.shape, 0)
+        made = lax.broadcasted_iota(jnp.int32, weave.shape, 1)
+        weave[...] = (taken == made // 2 + made % 2 * lanes).astype(jnp.float32).astype(jnp.bfloat16)
+
+    place = (lax.axis_index("wide") * 2 + lax.axis_index("core")) * pl.num_programs(0) + step
     real, imag = [], []
-    for source in (mine_rows, other_rows):
+    for source in rows:
         for x in range(wide):
-            first, second = source[0, x, 0], source[0, x, 1]
+            first, second = source[place, x, 0], source[place, x, 1]
             real += [first, second]
             imag += [second, -first]
-    for part, rows in ((0, real), (1, imag)):
-        value = lax.dot_general(
-            jnp.concatenate(rows, axis=0), side[...], DOWN, preferred_element_type=jnp.float32
-        )
-        out[:, part, :] = (value * scale).astype(jnp.bfloat16)
-
-
-def correlate(mine_rows, other_rows, mine_cols, other_cols, rotation, place, scale, own_rows):
-    blocks, wide, parts, spec, lanes = mine_cols.shape
-    own_blocks = own_rows // lanes
-    row_spec = pl.BlockSpec((1, wide, parts, spec, lanes), lambda i, place: (place[1] * own_blocks + i, 0, 0, 0, 0))
-    col_spec = pl.BlockSpec((blocks, wide, parts, spec, lanes), lambda i, place: (0, 0, 0, 0, 0))
+    both = jnp.concatenate([jnp.concatenate(real, axis=0), jnp.concatenate(imag, axis=0)], axis=1)
+    woven = jnp.dot(both, weave[...], preferred_element_type=jnp.float32)
+    exact = math.frexp(scale)[0] == 0.5
+    if exact:
+        woven *= scale
+    value = lax.dot_general(woven.astype(jnp.bfloat16), side[...], DOWN, preferred_element_type=jnp.float32)
+    if not exact:
+        value *= scale
+    out[...] = value.astype(jnp.bfloat16).reshape(out.shape)
+
+
+def correlate(sources, rotation, scale, own_rows):
+    blocks, wide, parts, spec, lanes = sources[0].shape
+    whole = pl.BlockSpec((blocks, wide, parts, spec, lanes), lambda i, rotation: (0, 0, 0, 0, 0))
     return pl.pallas_call(
         functools.partial(correlate_kernel, scale),
         grid_spec=pltpu.PrefetchScalarGridSpec(
             num_scalar_prefetch=1,
-            grid=(own_blocks,),
-            in_specs=[row_spec, row_spec, col_spec, col_spec],
-            out_specs=pl.BlockSpec((lanes, 2, blocks * lanes), lambda i, place: (i, 0, 0)),
-            scratch_shapes=[pltpu.VMEM((2 * wide * 2 * spec, blocks * lanes), jnp.bfloat16)],
+            grid=(own_rows // lanes,),
+            in_specs=[whole] * len(sources),
+            out_specs=pl.BlockSpec((lanes, 2, blocks * lanes), lambda i, rotation: (i, 0, 0)),
+            scratch_shapes=[
+                pltpu.VMEM((2 * wide * 2 * spec, blocks * lanes), jnp.bfloat16),
+                pltpu.VMEM((2 * lanes, 2 * lanes), jnp.bfloat16),
+            ],
         ),
         out_shape=jax.ShapeDtypeStruct((own_rows, 2, blocks * lanes), jnp.bfloat16),
         compiler_params=pltpu.CompilerParams(vmem_limit_bytes=56 * MIB, dimension_semantics=("arbitrary",)),
-    )(jnp.stack([rotation, place]), mine_rows, other_rows, mine_cols, other_cols)
+    )(rotation, *sources)
 
 
 def regroup(pieces, lanes):
@@ -333,13 +314,12 @@
     mine, other = mine.reshape(shape), other.reshape(shape)
     scale = 1.0 / math.sqrt(spec_local * time_count)
     own_rows = inputs // time_count
-    place = lax.axis_index(("wide", "core"))
     if aligned:
-        return correlate(mine, other, mine, other, offsets[0], place, scale, own_rows)[None]
+        return correlate((mine, other), offsets, scale, own_rows)[None]
     lanes = 256
     rows = [regroup(pieces, lanes) for pieces in (mine, other)]
     cols = [regroup(jnp.roll(pieces, -offsets[0], axis=0), lanes) for pieces in (mine, other)]
-    return correlate(*rows, *cols, offsets[0] * 0, place, scale, own_rows)[None]
+    return correlate((*rows, *cols), offsets * 0, scale, own_rows)[None]
 
 
 def solution(mesh):

time: 60.2 us -> 55.7 us (0.925)
  Pallas kernels: 32.9 us -> 28.4 us
  waiting for transfers between devices: 2.01 us -> 2.68 us
  other arithmetic: 1.65 us -> 0.99 us
    pallas_call x1, Pallas kernels: 27.4 us -> 23.9 us  [filterbank(): pl.pallas_call(functools.partial(filterbank_kernel, spec, rows), in_specs...]
    pallas_call x1, Pallas kernels: 5.53 us -> 4.49 us  [correlate(): pl.pallas_call(functools.partial(correlate_kernel, scale), grid_spec=pltp...]
    ppermute x1, waiting for transfers between devices: 0.87 us -> 1.53 us  [shards(): other = lax.ppermute(mine, 'core', [(0, 1), (1, 0)])]
    another operation x1 -> x0, other arithmetic: 0.67 us -> none  [correlate(): jnp.stack([rotation, place])]
  transfers between devices with their start and end apart: 2 -> 2, of which waited for: 2 -> 2; matrix products, arithmetic and copies ran while one was open for 1% -> 0% of each run, Pallas kernels for 0% -> 0%
where the time goes in v3:
time: 55.7 us; the launch traced here: 55.4 us
  Pallas kernels  28.4 us (51%)
  blocking collectives  19.6 us (35%)
  waiting for transfers between devices  2.68 us (5%)
  starting transfers between devices  2.35 us (4%)
  other arithmetic  0.99 us (2%)
  local copies, waits for them, and re-layouts  0.72 us (1%)
  between operations  0.71 us (1%)
    pallas_call x1, Pallas kernels, filterbank(): pl.pallas_call(functools.partial(filterbank_kernel, spec, rows), in_specs...  23.9 us
    all_to_all x1, blocking collectives, shards(): lax.all_to_all(sent, ('chan', 'wide'), split_axis=0, concat_axis=0, tiled...  19.6 us
    pallas_call x1, Pallas kernels, correlate(): pl.pallas_call(functools.partial(correlate_kernel, scale), grid_spec=pltp...  4.49 us
    ppermute x1, starting transfers between devices, shards(): lax.ppermute(tail, ('wide', 'core'), [(i, i + 1) for i in range(time_coun...  2.34 us
    ppermute x1, waiting for transfers between devices, shards(): other = lax.ppermute(mine, 'core', [(0, 1), (1, 0)])  1.53 us
    ppermute x1, waiting for transfers between devices, shards(): lax.ppermute(tail, ('wide', 'core'), [(i, i + 1) for i in range(time_coun...  1.15 us
  transfers between devices with their start and end apart: 2, of which 2 were waited for; matrix products, arithmetic and copies ran while one was open for 0% of the time, Pallas kernels for 0%

profile of v3, /device:TPU:0, one launch (start us, length us, event | category | flops | bytes accessed | tf_op | source)
XLA Modules:
  0.0 55.4 jit_solution(2623955949507169396)
XLA Ops:
  0.0 0.0 copy-start.2
  0.7 23.9 %shard_map.46 = (f32[16,16,256]{2,1,0:T(8,128)}, f32[16,7,256]{2,1,0:T(8,128)}) custom-call(s32[1]{0:T(128)S(6)} %copy.5.offset.rotation, f32[8,8192]{1,0:T(8,128)} %tap_hbm.1, bf16[256,131072]{1,0:T(8,128)(2,1)} %volt.1), custom_call_target="tpu_custom_call" | custom-call | flops 17179869184 | bytes 67108864 | tf_op jit(solution)/shard_map/pallas_call | solution.py:200
  24.6 2.3 %collective-permute-start = (f32[16,7,256]{2,1,0:T(8,128)}, f32[16,7,256]{2,1,0:T(8,128)S(1)}, u32[]{:S(2)}, u32[]{:S(2)}) collective-permute-start(f32[16,7,256]{2,1,0:T(8,128)} %get-tuple-element.8), channel_id=1, source_target_pairs={{0,1},{1,2},{2,3},{4,5},{5,6},{6,7},{8,9},{9,10},{10,11},{12,13},{... | collective-permute-start | bytes 344072 | tf_op jit(solution)/shard_map/ppermute | solution.py:305
  26.9 0.0 copy-done.2
  27.0 1.1 %collective-permute-done = f32[16,7,256]{2,1,0:T(8,128)S(1)} collective-permute-done((f32[16,7,256]{2,1,0:T(8,128)}, f32[16,7,256]{2,1,0:T(8,128)S(1)}, u32[]{:S(2)}, u32[]{:S(2)}) %collective-permute-start) | collective-permute-done | bytes 114720 | tf_op jit(solution)/shard_map/ppermute | solution.py:305
  28.1 1.0 %multiply_convert_fusion = bf16[16,16,256]{2,1,0:T(8,128)(2,1)S(1)} fusion(f32[16,16,256]{2,1,0:T(8,128)} %get-tuple-element.7, f32[16,7,256]{2,1,0:T(8,128)S(1)} %collective-permute-done, f32[16,256]{1,0:T(8,128)S(1)} %convert_bitcast_fusion), kind=kLoop, calls=%fused_computation | loop fusion | flops 196608 | bytes 524288 | tf_op jit(solution)/shard_map/convert_element_type | solution.py:307
  29.1 19.6 %all_to_all.5 = bf16[16,2,16,256]{3,2,1,0:T(8,128)(2,1)S(1)} all-to-all(bf16[16,2,16,256]{3,2,1,0:T(8,128)(2,1)S(1)} %bitcast.8), channel_id=1, replica_groups=mesh['chan'=8,'wide'=2,'core'=2] {'chan','wide'}, dimensions={0} | all-to-all | bytes 524288 | tf_op jit(solution)/shard_map/all_to_all | solution.py:311
  48.7 0.0 copy-start
  48.7 0.0 collective-permute-start.1
  48.7 1.5 %collective-permute-done.1 = bf16[16,2,16,256]{3,2,1,0:T(8,128)(2,1)S(1)} collective-permute-done((bf16[16,2,16,256]{3,2,1,0:T(8,128)(2,1)S(1)}, bf16[16,2,16,256]{3,2,1,0:T(8,128)(2,1)S(1)}, u32[]{:S(2)}, u32[]{:S(2)}) %collective-permute-start.1) | collective-permute-done | bytes 262176 | tf_op jit(solution)/shard_map/ppermute | solution.py:312
  50.2 0.0 copy-start.1
  50.2 0.0 copy-done
  50.2 0.7 %copy-done.1 = bf16[16,2,16,256]{3,2,1,0:T(8,128)(2,1)} copy-done((bf16[16,2,16,256]{3,2,1,0:T(8,128)(2,1)}, bf16[16,2,16,256]{3,2,1,0:T(8,128)(2,1)S(1)}, u32[]{:S(2)}) %copy-start.1) | copy-done | bytes 262168
  50.9 4.5 %shard_map.47 = bf16[512,2,2048]{2,1,0:T(2,128)(2,1)} custom-call(s32[1]{0:T(128)S(6)} %copy.5.offset.rotation, bf16[8,2,2,16,256]{4,3,2,1,0:T(8,128)(2,1)} %bitcast.7, bf16[8,2,2,16,256]{4,3,2,1,0:T(8,128)(2,1)} %bitcast.10), custom_call_target="tpu_custom_call" | custom-call | tf_op jit(solution)/shard_map/pallas_call | solution.py:267
  (2 shorter events, 0.0 us)
Async XLA Ops:
  0.0 26.9 %copy-start.2 = (s32[256,16]{0,1:T(8,128)S(1)}, s32[256,16]{0,1:T(8,128)}, u32[]{:S(2)}) copy-start(s32[256,16]{0,1:T(8,128)} %param.6) | copy-start | bytes 49156
  24.6 3.5 %collective-permute-start = (f32[16,7,256]{2,1,0:T(8,128)}, f32[16,7,256]{2,1,0:T(8,128)S(1)}, u32[]{:S(2)}, u32[]{:S(2)}) collective-permute-start(f32[16,7,256]{2,1,0:T(8,128)} %get-tuple-element.8), channel_id=1, source_target_pairs={{0,1},{1,2},{2,3},{4,5},{5,6},{6,7},{8,9},{9,10},{10,11},{12,13},{... | collective-permute-start | bytes 344072 | tf_op jit(solution)/shard_map/ppermute | solution.py:305
  48.7 1.5 %copy-start = (bf16[16,2,16,256]{3,2,1,0:T(8,128)(2,1)}, bf16[16,2,16,256]{3,2,1,0:T(8,128)(2,1)S(1)}, u32[]{:S(2)}) copy-start(bf16[16,2,16,256]{3,2,1,0:T(8,128)(2,1)S(1)} %all_to_all.5) | copy-start | bytes 786436
  48.7 1.5 %collective-permute-start.1 = (bf16[16,2,16,256]{3,2,1,0:T(8,128)(2,1)S(1)}, bf16[16,2,16,256]{3,2,1,0:T(8,128)(2,1)S(1)}, u32[]{:S(2)}, u32[]{:S(2)}) collective-permute-start(bf16[16,2,16,256]{3,2,1,0:T(8,128)(2,1)S(1)} %all_to_all.5), channel_id=1, source_target_pairs={{0,1},{1,0},{2,3},{3,2},{4,5},{5,4},{6,7},{7,6},{8,9},{9,8},{10,11... | collective-permute-start | bytes 786440 | tf_op jit(solution)/shard_map/ppermute | solution.py:312
  50.2 0.7 %copy-start.1 = (bf16[16,2,16,256]{3,2,1,0:T(8,128)(2,1)}, bf16[16,2,16,256]{3,2,1,0:T(8,128)(2,1)S(1)}, u32[]{:S(2)}) copy-start(bf16[16,2,16,256]{3,2,1,0:T(8,128)(2,1)S(1)} %collective-permute-done.1) | copy-start | bytes 786436

commit v4 on v3

--- a/solution.py
+++ b/solution.py
@@ -201,9 +201,10 @@
         functools.partial(filterbank_kernel, spec, rows),
         in_specs=[
             pl.BlockSpec(memory_space=pltpu.SMEM),
-            pl.BlockSpec(memory_space=pl.ANY),
-            pl.BlockSpec(memory_space=pl.ANY),
-        ],
+            pl.BlockSpec(memory_space=pltpu.HBM),
+            pl.BlockSpec(memory_space=pltpu.HBM),
+        ],
+        out_specs=[pl.BlockSpec(memory_space=pltpu.VMEM)] * 2,
         out_shape=[
             jax.ShapeDtypeStruct((pairs, spec, rows), jnp.float32),
             jax.ShapeDtypeStruct((pairs, count - 1, rows), jnp.float32),
@@ -216,7 +217,7 @@
             pltpu.SemaphoreType.DMA((AHEAD + 1,)),
             pltpu.SemaphoreType.DMA,
         ],
-        compiler_params=pltpu.CompilerParams(vmem_limit_bytes=56 * MIB),
+        compiler_params=pltpu.CompilerParams(vmem_limit_bytes=36 * MIB),
         cost_estimate=pl.CostEstimate(
             flops=4 * spec * rows * frame * cols, bytes_accessed=2 * rows * width, transcendentals=0
         ),
@@ -263,7 +264,7 @@
 
 def correlate(sources, rotation, scale, own_rows):
     blocks, wide, parts, spec, lanes = sources[0].shape
-    whole = pl.BlockSpec((blocks, wide, parts, spec, lanes), lambda i, rotation: (0, 0, 0, 0, 0))
+    whole = pl.BlockSpec(memory_space=pltpu.VMEM)
     return pl.pallas_call(
         functools.partial(correlate_kernel, scale),
         grid_spec=pltpu.PrefetchScalarGridSpec(
@@ -277,7 +278,7 @@
             ],
         ),
         out_shape=jax.ShapeDtypeStruct((own_rows, 2, blocks * lanes), jnp.bfloat16),
-        compiler_params=pltpu.CompilerParams(vmem_limit_bytes=56 * MIB, dimension_semantics=("arbitrary",)),
+        compiler_params=pltpu.CompilerParams(vmem_limit_bytes=24 * MIB, dimension_semantics=("arbitrary",)),
     )(rotation, *sources)
 
 

time: 55.7 us -> 52.9 us (0.950)
  Pallas kernels: 28.4 us -> 26.5 us
  other arithmetic: 0.99 us -> 0.04 us
    pallas_call x1, Pallas kernels: 4.49 us -> 3.44 us  [correlate(): pl.pallas_call(functools.partial(correlate_kernel, scale), grid_spec=pltp...]
    convert_element_type x1, other arithmetic: 0.98 us -> 0.03 us  [shards(): (spectrum * flags.astype(jnp.float32).T[None]).astype(jnp.bfloat16)]
    pallas_call x1, Pallas kernels: 23.9 us -> 23.1 us  [filterbank(): pl.pallas_call(functools.partial(filterbank_kernel, spec, rows), in_specs...]
where the time goes in v4:
time: 52.9 us; the launch traced here: 52.7 us
  Pallas kernels  26.5 us (50%)
  blocking collectives  19.6 us (37%)
  waiting for transfers between devices  2.47 us (5%)
  starting transfers between devices  2.36 us (4%)
  local copies, waits for them, and re-layouts  0.97 us (2%)
  between operations  0.71 us (1%)
    pallas_call x1, Pallas kernels, filterbank(): pl.pallas_call(functools.partial(filterbank_kernel, spec, rows), in_specs...  23.1 us
    all_to_all x1, blocking collectives, shards(): lax.all_to_all(sent, ('chan', 'wide'), split_axis=0, concat_axis=0, tiled...  19.6 us
    pallas_call x1, Pallas kernels, correlate(): pl.pallas_call(functools.partial(correlate_kernel, scale), grid_spec=pltp...  3.44 us
    ppermute x1, starting transfers between devices, shards(): lax.ppermute(tail, ('wide', 'core'), [(i, i + 1) for i in range(time_coun...  2.35 us
    ppermute x1, waiting for transfers between devices, shards(): other = lax.ppermute(mine, 'core', [(0, 1), (1, 0)])  1.53 us
  transfers between devices with their start and end apart: 2, of which 2 were waited for; matrix products, arithmetic and copies ran while one was open for 0% of the time, Pallas kernels for 0%

profile of v4, /device:TPU:0, one launch (start us, length us, event | category | flops | bytes accessed | tf_op | source)
XLA Modules:
  0.0 52.7 jit_solution(2633741503338601879)
XLA Ops:
  0.7 0.0 copy-start
  0.7 0.9 %copy-done = f32[8,8192]{1,0:T(8,128)S(1)} copy-done((f32[8,8192]{1,0:T(8,128)S(1)}, f32[8,8192]{1,0:T(8,128)}, u32[]{:S(2)}) %copy-start) | copy-done | bytes 262168
  1.6 0.0 copy-start.1
  1.6 23.1 %shard_map.46 = (f32[16,16,256]{2,1,0:T(8,128)S(1)}, f32[16,7,256]{2,1,0:T(8,128)S(1)}) custom-call(s32[1]{0:T(128)S(6)} %copy.5.offset.rotation, f32[8,8192]{1,0:T(8,128)S(1)} %copy-done, bf16[256,131072]{1,0:T(8,128)(2,1)} %volt.1), custom_call_target="tpu_custom_call" | custom-call | flops 17179869184 | bytes 67108864 | tf_op jit(solution)/shard_map/pallas_call | solution.py:200
  24.7 2.4 %collective-permute-start = (f32[16,7,256]{2,1,0:T(8,128)S(1)}, f32[16,7,256]{2,1,0:T(8,128)S(1)}, u32[]{:S(2)}, u32[]{:S(2)}) collective-permute-start(f32[16,7,256]{2,1,0:T(8,128)S(1)} %get-tuple-element.8), channel_id=1, source_target_pairs={{0,1},{1,2},{2,3},{4,5},{5,6},{6,7},{8,9},{9,10},{10,11},{12,13},{... | collective-permute-start | bytes 344072 | tf_op jit(solution)/shard_map/ppermute | solution.py:306
  27.1 0.0 copy-done.1
  27.1 0.9 %collective-permute-done = f32[16,7,256]{2,1,0:T(8,128)S(1)} collective-permute-done((f32[16,7,256]{2,1,0:T(8,128)S(1)}, f32[16,7,256]{2,1,0:T(8,128)S(1)}, u32[]{:S(2)}, u32[]{:S(2)}) %collective-permute-start) | collective-permute-done | bytes 114720 | tf_op jit(solution)/shard_map/ppermute | solution.py:306
  28.1 19.6 %all_to_all.5 = bf16[16,2,16,256]{3,2,1,0:T(8,128)(2,1)S(1)} all-to-all(bf16[16,2,16,256]{3,2,1,0:T(8,128)(2,1)S(1)} %bitcast.9), channel_id=1, replica_groups=mesh['chan'=8,'wide'=2,'core'=2] {'chan','wide'}, dimensions={0} | all-to-all | bytes 524288 | tf_op jit(solution)/shard_map/all_to_all | solution.py:312
  47.7 0.0 collective-permute-start.1
  47.7 1.5 %collective-permute-done.1 = bf16[16,2,16,256]{3,2,1,0:T(8,128)(2,1)S(1)} collective-permute-done((bf16[16,2,16,256]{3,2,1,0:T(8,128)(2,1)S(1)}, bf16[16,2,16,256]{3,2,1,0:T(8,128)(2,1)S(1)}, u32[]{:S(2)}, u32[]{:S(2)}) %collective-permute-start.1) | collective-permute-done | bytes 262176 | tf_op jit(solution)/shard_map/ppermute | solution.py:313
  49.2 3.4 %shard_map.47 = bf16[512,2,2048]{2,1,0:T(2,128)(2,1)} custom-call(s32[1]{0:T(128)S(6)} %copy.5.offset.rotation, bf16[8,2,2,16,256]{4,3,2,1,0:T(8,128)(2,1)S(1)} %bitcast.7, bf16[8,2,2,16,256]{4,3,2,1,0:T(8,128)(2,1)S(1)} %bitcast.8), custom_call_target="tpu_custom_call" | custom-call | tf_op jit(solution)/shard_map/pallas_call | solution.py:268
  (3 shorter events, 0.1 us)
Async XLA Ops:
  0.7 1.0 %copy-start = (f32[8,8192]{1,0:T(8,128)S(1)}, f32[8,8192]{1,0:T(8,128)}, u32[]{:S(2)}) copy-start(f32[8,8192]{1,0:T(8,128)} %tap_hbm.1) | copy-start | bytes 786436
  1.6 25.5 %copy-start.1 = (s32[256,16]{0,1:T(8,128)S(1)}, s32[256,16]{0,1:T(8,128)}, u32[]{:S(2)}) copy-start(s32[256,16]{0,1:T(8,128)} %param.6) | copy-start | bytes 49156
  24.7 3.3 %collective-permute-start = (f32[16,7,256]{2,1,0:T(8,128)S(1)}, f32[16,7,256]{2,1,0:T(8,128)S(1)}, u32[]{:S(2)}, u32[]{:S(2)}) collective-permute-start(f32[16,7,256]{2,1,0:T(8,128)S(1)} %get-tuple-element.8), channel_id=1, source_target_pairs={{0,1},{1,2},{2,3},{4,5},{5,6},{6,7},{8,9},{9,10},{10,11},{12,13},{... | collective-permute-start | bytes 344072 | tf_op jit(solution)/shard_map/ppermute | solution.py:306
  47.7 1.5 %collective-permute-start.1 = (bf16[16,2,16,256]{3,2,1,0:T(8,128)(2,1)S(1)}, bf16[16,2,16,256]{3,2,1,0:T(8,128)(2,1)S(1)}, u32[]{:S(2)}, u32[]{:S(2)}) collective-permute-start(bf16[16,2,16,256]{3,2,1,0:T(8,128)(2,1)S(1)} %all_to_all.5), channel_id=1, source_target_pairs={{0,1},{1,0},{2,3},{3,2},{4,5},{5,4},{6,7},{7,6},{8,9},{9,8},{10,11... | collective-permute-start | bytes 786440 | tf_op jit(solution)/shard_map/ppermute | solution.py:313

commit v5 on v4

--- a/solution.py
+++ b/solution.py
@@ -217,7 +217,7 @@
             pltpu.SemaphoreType.DMA((AHEAD + 1,)),
             pltpu.SemaphoreType.DMA,
         ],
-        compiler_params=pltpu.CompilerParams(vmem_limit_bytes=36 * MIB),
+        compiler_params=pltpu.CompilerParams(vmem_limit_bytes=107 * MIB // 2),
         cost_estimate=pl.CostEstimate(
             flops=4 * spec * rows * frame * cols, bytes_accessed=2 * rows * width, transcendentals=0
         ),

time: 52.9 us -> 52 us (0.983)
  local copies, waits for them, and re-layouts: 0.97 us -> 0.02 us
    unnamed x4 -> x2, local copies, waits for them, and re-layouts: 0.95 us -> 0.01 us
where the time goes in v5:
time: 52 us; the launch traced here: 51.8 us
  Pallas kernels  26.6 us (51%)
  blocking collectives  19.6 us (38%)
  waiting for transfers between devices  2.47 us (5%)
  starting transfers between devices  2.35 us (5%)
  between operations  0.71 us (1%)
    pallas_call x1, Pallas kernels, filterbank(): pl.pallas_call(functools.partial(filterbank_kernel, spec, rows), in_specs...  23.2 us
    all_to_all x1, blocking collectives, shards(): lax.all_to_all(sent, ('chan', 'wide'), split_axis=0, concat_axis=0, tiled...  19.6 us
    pallas_call x1, Pallas kernels, correlate(): pl.pallas_call(functools.partial(correlate_kernel, scale), grid_spec=pltp...  3.44 us
    ppermute x1, starting transfers between devices, shards(): lax.ppermute(tail, ('wide', 'core'), [(i, i + 1) for i in range(time_coun...  2.35 us
    ppermute x1, waiting for transfers between devices, shards(): other = lax.ppermute(mine, 'core', [(0, 1), (1, 0)])  1.53 us
  transfers between devices with their start and end apart: 2, of which 2 were waited for; matrix products, arithmetic and copies ran while one was open for 0% of the time, Pallas kernels for 0%

profile of v5, /device:TPU:0, one launch (start us, length us, event | category | flops | bytes accessed | tf_op | source)
XLA Modules:
  0.0 51.8 jit_solution(13530938614226080411)
XLA Ops:
  0.0 0.0 copy-start
  0.7 23.2 %shard_map.46 = (f32[16,16,256]{2,1,0:T(8,128)S(1)}, f32[16,7,256]{2,1,0:T(8,128)S(1)}) custom-call(s32[1]{0:T(128)S(6)} %copy.5.offset.rotation, f32[8,8192]{1,0:T(8,128)} %tap_hbm.1, bf16[256,131072]{1,0:T(8,128)(2,1)} %volt.1), custom_call_target="tpu_custom_call" | custom-call | flops 17179869184 | bytes 67108864 | tf_op jit(solution)/shard_map/pallas_call | solution.py:200
  23.8 2.4 %collective-permute-start = (f32[16,7,256]{2,1,0:T(8,128)S(1)}, f32[16,7,256]{2,1,0:T(8,128)S(1)}, u32[]{:S(2)}, u32[]{:S(2)}) collective-permute-start(f32[16,7,256]{2,1,0:T(8,128)S(1)} %get-tuple-element.8), channel_id=1, source_target_pairs={{0,1},{1,2},{2,3},{4,5},{5,6},{6,7},{8,9},{9,10},{10,11},{12,13},{... | collective-permute-start | bytes 344072 | tf_op jit(solution)/shard_map/ppermute | solution.py:306
  26.2 0.0 copy-done
  26.2 0.9 %collective-permute-done = f32[16,7,256]{2,1,0:T(8,128)S(1)} collective-permute-done((f32[16,7,256]{2,1,0:T(8,128)S(1)}, f32[16,7,256]{2,1,0:T(8,128)S(1)}, u32[]{:S(2)}, u32[]{:S(2)}) %collective-permute-start) | collective-permute-done | bytes 114720 | tf_op jit(solution)/shard_map/ppermute | solution.py:306
  27.2 19.6 %all_to_all.5 = bf16[16,2,16,256]{3,2,1,0:T(8,128)(2,1)S(1)} all-to-all(bf16[16,2,16,256]{3,2,1,0:T(8,128)(2,1)S(1)} %bitcast.9), channel_id=1, replica_groups=mesh['chan'=8,'wide'=2,'core'=2] {'chan','wide'}, dimensions={0} | all-to-all | bytes 524288 | tf_op jit(solution)/shard_map/all_to_all | solution.py:312
  46.8 0.0 collective-permute-start.1
  46.8 1.5 %collective-permute-done.1 = bf16[16,2,16,256]{3,2,1,0:T(8,128)(2,1)S(1)} collective-permute-done((bf16[16,2,16,256]{3,2,1,0:T(8,128)(2,1)S(1)}, bf16[16,2,16,256]{3,2,1,0:T(8,128)(2,1)S(1)}, u32[]{:S(2)}, u32[]{:S(2)}) %collective-permute-start.1) | collective-permute-done | bytes 262176 | tf_op jit(solution)/shard_map/ppermute | solution.py:313
  48.3 3.4 %shard_map.47 = bf16[512,2,2048]{2,1,0:T(2,128)(2,1)} custom-call(s32[1]{0:T(128)S(6)} %copy.5.offset.rotation, bf16[8,2,2,16,256]{4,3,2,1,0:T(8,128)(2,1)S(1)} %bitcast.7, bf16[8,2,2,16,256]{4,3,2,1,0:T(8,128)(2,1)S(1)} %bitcast.8), custom_call_target="tpu_custom_call" | custom-call | tf_op jit(solution)/shard_map/pallas_call | solution.py:268
  (3 shorter events, 0.1 us)
Async XLA Ops:
  0.0 26.2 %copy-start = (s32[256,16]{0,1:T(8,128)S(1)}, s32[256,16]{0,1:T(8,128)}, u32[]{:S(2)}) copy-start(s32[256,16]{0,1:T(8,128)} %param.6) | copy-start | bytes 49156
  23.8 3.3 %collective-permute-start = (f32[16,7,256]{2,1,0:T(8,128)S(1)}, f32[16,7,256]{2,1,0:T(8,128)S(1)}, u32[]{:S(2)}, u32[]{:S(2)}) collective-permute-start(f32[16,7,256]{2,1,0:T(8,128)S(1)} %get-tuple-element.8), channel_id=1, source_target_pairs={{0,1},{1,2},{2,3},{4,5},{5,6},{6,7},{8,9},{9,10},{10,11},{12,13},{... | collective-permute-start | bytes 344072 | tf_op jit(solution)/shard_map/ppermute | solution.py:306
  46.8 1.5 %collective-permute-start.1 = (bf16[16,2,16,256]{3,2,1,0:T(8,128)(2,1)S(1)}, bf16[16,2,16,256]{3,2,1,0:T(8,128)(2,1)S(1)}, u32[]{:S(2)}, u32[]{:S(2)}) collective-permute-start(bf16[16,2,16,256]{3,2,1,0:T(8,128)(2,1)S(1)} %all_to_all.5), channel_id=1, source_target_pairs={{0,1},{1,0},{2,3},{3,2},{4,5},{5,4},{6,7},{7,6},{8,9},{9,8},{10,11... | collective-permute-start | bytes 786440 | tf_op jit(solution)/shard_map/ppermute | solution.py:313

commit v6 on v5

--- a/solution.py
+++ b/solution.py
@@ -12,8 +12,9 @@
 MIB = 1024 * 1024
 ACROSS = (((1,), (1,)), ((), ()))
 DOWN = (((0,), (0,)), ((), ()))
-GROUP = 1
 AHEAD = 3
+READY = 2
+LATE = 9
 
 
 def channel_table(frame, channels, width, shift):
@@ -124,41 +125,53 @@
     )(table, taps, volt)
 
 
-def filterbank_kernel(spec, rows, offset, tap_hbm, volt, own, tail, tap_ref, held, weights, folded, sems, tap_sem):
+def frame_copy(volt, f, target, sem):
+    frame = target.shape[-1]
+    return pltpu.make_async_copy(volt.at[:, pl.ds(pl.multiple_of(f * frame, frame), frame)], target, sem)
+
+
+def add_frame(weights, block, folded, f, pairs):
+    value = lax.dot_general(weights[...], block[...], ACROSS, preferred_element_type=jnp.float32)
+    rows = value.shape[1]
+    cols = value.shape[0] // 2
+    value = value[:cols] + value[cols:]
+    for t in range(cols // pairs):
+        span = pl.ds(pl.multiple_of((f + t) * rows, rows), rows)
+        folded[:, span] += value[t * pairs : (t + 1) * pairs, :]
+
+
+def late_kernel(spec, rows, offset, tap_ref, volt, tail, partial, weights, ready, held, folded, sems, ready_sems):
     taps, frame = tap_ref.shape
-    pairs = own.shape[0]
+    pairs = partial.shape[0]
     cols = taps * pairs
     ring = held.shape[0]
-    steps = spec // GROUP
+    first, count, history = spec - LATE, LATE, taps - 1
     strip = 512
 
-    def copies(step):
-        slot = lax.rem(step, ring)
-        made = []
-        for n in range(GROUP):
-            start = pl.multiple_of((step * GROUP + n) * frame, frame)
-            made.append(
-                pltpu.make_async_copy(
-                    volt.at[:, pl.ds(start, frame)], held.at[slot, pl.ds(n * rows, rows), :], sems.at[slot]
-                )
-            )
-        return made
-
-    taps_copy = pltpu.make_async_copy(tap_hbm, tap_ref, tap_sem)
-    taps_copy.start()
-
-    @pl.loop(0, AHEAD)
-    def _(step):
-        for copy in copies(step):
-            copy.start()
-
+    def start(step):
+        @pl.when(step < count)
+        def _():
+            slot = lax.rem(step, ring)
+            frame_copy(volt, first + step, held.at[slot], sems.at[slot]).start()
+
+        @pl.when((step >= count) & (step < count + READY))
+        def _():
+            f = step - count
+            frame_copy(volt, f, ready.at[f], ready_sems.at[f]).start()
+
+    strips = frame // strip
+    stage = strips // (AHEAD - 1)
+    start(jnp.int32(0))
     folded[...] = jnp.zeros_like(folded)
     table = channel_table(frame, pairs // 2, 128, jnp.minimum(offset[0], 0))
     table = jnp.concatenate([table] * (strip // 128), axis=1)
-    taps_copy.wait()
-
-    @pl.loop(0, frame // strip)
+
+    @pl.loop(0, strips)
     def _(s):
+        @pl.when(lax.rem(s + 1, stage) == 0)
+        def _():
+            start((s + 1) // stage)
+
         span = pl.ds(pl.multiple_of(s * strip, strip), strip)
         for t in range(taps):
             exact = tap_ref[t : t + 1, span] * table
@@ -167,29 +180,52 @@
             weights[t * pairs : (t + 1) * pairs, span] = high
             weights[cols + t * pairs : cols + (t + 1) * pairs, span] = low
 
-    @pl.loop(0, steps)
+    @pl.loop(0, count)
     def _(step):
         slot = lax.rem(step, ring)
-        block = held.at[slot]
-        pltpu.make_async_copy(block, block, sems.at[slot]).wait()
-
-        @pl.when(step + AHEAD < steps)
+        pltpu.make_async_copy(held.at[slot], held.at[slot], sems.at[slot]).wait()
+        start(step + AHEAD)
+        add_frame(weights, held.at[slot], folded, first + step, pairs)
+
+    for f in range(history):
+        tail[:, f, :] = folded[:, (spec + f) * rows : (spec + f + 1) * rows]
+    partial[...] = folded[:, : spec * rows]
+
+    for f in range(READY):
+        pltpu.make_async_copy(ready.at[f], ready.at[f], ready_sems.at[f]).wait()
+
+
+def early_kernel(spec, rows, weights, ready, partial, volt, own, held, folded, sems):
+    frame = weights.shape[1]
+    pairs = partial.shape[0]
+    ring = held.shape[0]
+    count = spec - LATE - READY
+
+    def start(step):
+        @pl.when(step < count)
         def _():
-            for copy in copies(step + AHEAD):
-                copy.start()
-
-        value = lax.dot_general(weights[...], block[...], ACROSS, preferred_element_type=jnp.float32)
-        value = value[:cols] + value[cols:]
-        for t in range(taps):
-            span = pl.ds(pl.multiple_of((step * GROUP + t) * rows, rows), GROUP * rows)
-            folded[:, span] += value[t * pairs : (t + 1) * pairs, :]
-
-    for f in range(spec + taps - 1):
-        value = folded[:, f * rows : (f + 1) * rows]
-        if f < spec:
-            own[:, f, :] = value
-        else:
-            tail[:, f - spec, :] = value
+            slot = lax.rem(step, ring)
+            frame_copy(volt, READY + step, held.at[slot], sems.at[slot]).start()
+
+    @pl.loop(0, AHEAD)
+    def _(step):
+        start(step)
+
+    folded[...] = partial[...]
+
+    @pl.loop(0, READY)
+    def _(f):
+        add_frame(weights, ready.at[f], folded, f, pairs)
+
+    @pl.loop(0, count)
+    def _(step):
+        slot = lax.rem(step, ring)
+        pltpu.make_async_copy(held.at[slot], held.at[slot], sems.at[slot]).wait()
+        start(step + AHEAD)
+        add_frame(weights, held.at[slot], folded, READY + step, pairs)
+
+    for f in range(spec):
+        own[:, f, :] = folded[:, f * rows : (f + 1) * rows]
 
 
 def filterbank(volt, taps, offsets, channels, spec):
@@ -197,31 +233,46 @@
     count, frame = taps.shape
     pairs = 2 * channels
     cols = count * pairs
-    return pl.pallas_call(
-        functools.partial(filterbank_kernel, spec, rows),
-        in_specs=[
-            pl.BlockSpec(memory_space=pltpu.SMEM),
-            pl.BlockSpec(memory_space=pltpu.HBM),
-            pl.BlockSpec(memory_space=pltpu.HBM),
-        ],
-        out_specs=[pl.BlockSpec(memory_space=pltpu.VMEM)] * 2,
+    vmem, hbm = pl.BlockSpec(memory_space=pltpu.VMEM), pl.BlockSpec(memory_space=pl.ANY)
+
+    def cost(frames):
+        return pl.CostEstimate(
+            flops=4 * frames * rows * frame * cols, bytes_accessed=2 * frames * rows * frame, transcendentals=0
+        )
+
+    tail, partial, weights, ready = pl.pallas_call(
+        functools.partial(late_kernel, spec, rows),
+        in_specs=[pl.BlockSpec(memory_space=pltpu.SMEM), vmem, hbm],
+        out_specs=[vmem] * 4,
         out_shape=[
-            jax.ShapeDtypeStruct((pairs, spec, rows), jnp.float32),
             jax.ShapeDtypeStruct((pairs, count - 1, rows), jnp.float32),
+            jax.ShapeDtypeStruct((pairs, spec * rows), jnp.float32),
+            jax.ShapeDtypeStruct((2 * cols, frame), jnp.bfloat16),
+            jax.ShapeDtypeStruct((READY, rows, frame), jnp.bfloat16),
         ],
         scratch_shapes=[
-            pltpu.VMEM((count, frame), jnp.float32),
-            pltpu.VMEM((AHEAD + 1, GROUP * rows, frame), jnp.bfloat16),
-            pltpu.VMEM((2 * cols, frame), jnp.bfloat16),
+            pltpu.VMEM((AHEAD + 1, rows, frame), jnp.bfloat16),
             pltpu.VMEM((pairs, (spec + count - 1) * rows), jnp.float32),
             pltpu.SemaphoreType.DMA((AHEAD + 1,)),
-            pltpu.SemaphoreType.DMA,
-        ],
-        compiler_params=pltpu.CompilerParams(vmem_limit_bytes=107 * MIB // 2),
-        cost_estimate=pl.CostEstimate(
-            flops=4 * spec * rows * frame * cols, bytes_accessed=2 * rows * width, transcendentals=0
-        ),
+            pltpu.SemaphoreType.DMA((READY,)),
+        ],
+        compiler_params=pltpu.CompilerParams(vmem_limit_bytes=24 * MIB),
+        cost_estimate=cost(LATE),
     )(offsets, taps, volt)
+    own = pl.pallas_call(
+        functools.partial(early_kernel, spec, rows),
+        in_specs=[vmem, vmem, vmem, hbm],
+        out_specs=vmem,
+        out_shape=jax.ShapeDtypeStruct((pairs, spec, rows), jnp.float32),
+        scratch_shapes=[
+            pltpu.VMEM((AHEAD + 1, rows, frame), jnp.bfloat16),
+            pltpu.VMEM((pairs, spec * rows), jnp.float32),
+            pltpu.SemaphoreType.DMA((AHEAD + 1,)),
+        ],
+        compiler_params=pltpu.CompilerParams(vmem_limit_bytes=24 * MIB),
+        cost_estimate=cost(spec - LATE),
+    )(weights, ready, partial, volt)
+    return own, tail
 
 
 def correlate_kernel(scale, rotation, *refs):

time: 52 us -> 51.4 us (0.988)
  blocking collectives: 19.6 us -> 18.4 us
  local copies, waits for them, and re-layouts: 0.02 us -> 0.97 us
  waiting for transfers between devices: 2.47 us -> 1.54 us
    all_to_all x1, blocking collectives: 19.6 us -> 18.4 us  [shards(): lax.all_to_all(sent, ('chan', 'wide'), split_axis=0, concat_axis=0, tiled...]
    unnamed x2 -> x4, local copies, waits for them, and re-layouts: 0.01 us -> 0.95 us
    ppermute x1, waiting for transfers between devices: 0.94 us -> 0.01 us  [shards(): lax.ppermute(tail, ('wide', 'core'), [(i, i + 1) for i in range(time_coun...]
    pallas_call x1 -> x2, Pallas kernels: 23.2 us -> 23.7 us  [the longest x1 14.5 us: filterbank(): pl.pallas_call(functools.partial(late_kernel, spec, rows), in_specs=[pl.B...]
  transfers between devices with their start and end apart: 2 -> 2, of which waited for: 2 -> 1; matrix products, arithmetic and copies ran while one was open for 0% -> 0% of each run, Pallas kernels for 0% -> 18%
where the time goes in v6:
time: 51.4 us; the launch traced here: 51.2 us
  Pallas kernels  27.1 us (53%)
  blocking collectives  18.4 us (36%)
  starting transfers between devices  2.37 us (5%)
  waiting for transfers between devices  1.54 us (3%)
  local copies, waits for them, and re-layouts  0.97 us (2%)
  between operations  0.73 us (1%)
    all_to_all x1, blocking collectives, shards(): lax.all_to_all(sent, ('chan', 'wide'), split_axis=0, concat_axis=0, tiled...  18.4 us
    pallas_call x1, Pallas kernels, filterbank(): pl.pallas_call(functools.partial(late_kernel, spec, rows), in_specs=[pl.B...  14.5 us
    pallas_call x1, Pallas kernels, filterbank(): pl.pallas_call(functools.partial(early_kernel, spec, rows), in_specs=[vme...  9.22 us
    pallas_call x1, Pallas kernels, correlate(): pl.pallas_call(functools.partial(correlate_kernel, scale), grid_spec=pltp...  3.44 us
    ppermute x1, starting transfers between devices, shards(): lax.ppermute(tail, ('wide', 'core'), [(i, i + 1) for i in range(time_coun...  2.36 us
    ppermute x1, waiting for transfers between devices, shards(): other = lax.ppermute(mine, 'core', [(0, 1), (1, 0)])  1.53 us
  transfers between devices with their start and end apart: 2, of which 1 were waited for; matrix products, arithmetic and copies ran while one was open for 0% of the time, Pallas kernels for 18%

profile of v6, /device:TPU:0, one launch (start us, length us, event | category | flops | bytes accessed | tf_op | source)
XLA Modules:
  0.0 51.2 jit_solution(17390673821623225675)
XLA Ops:
  0.7 0.0 copy-start
  0.7 0.9 %copy-done = f32[8,8192]{1,0:T(8,128)S(1)} copy-done((f32[8,8192]{1,0:T(8,128)S(1)}, f32[8,8192]{1,0:T(8,128)}, u32[]{:S(2)}) %copy-start) | copy-done | bytes 262168
  1.6 14.5 %shard_map.46 = (f32[16,7,256]{2,1,0:T(8,128)S(1)}, f32[16,4096]{1,0:T(8,128)S(1)}, bf16[256,8192]{1,0:T(8,128)(2,1)S(1)}, bf16[2,256,8192]{2,1,0:T(8,128)(2,1)S(1)}) custom-call(s32[1]{0:T(128)S(6)} %copy.5.offset.rotation, f32[8,8192]{1,0:T(8,128)S(1)} %copy-done, bf16[256,131072]{1,0:T(8,128)(2,1)} %volt.3), custom_call_target="tpu_custom_call" | custom-call | flops 9663676416 | bytes 37748736 | tf_op jit(solution)/shard_map/pallas_call | solution.py:243
  16.1 2.4 %collective-permute-start = (f32[16,7,256]{2,1,0:T(8,128)S(1)}, f32[16,7,256]{2,1,0:T(8,128)S(1)}, u32[]{:S(2)}, u32[]{:S(2)}) collective-permute-start(f32[16,7,256]{2,1,0:T(8,128)S(1)} %get-tuple-element.12), channel_id=1, source_target_pairs={{0,1},{1,2},{2,3},{4,5},{5,6},{6,7},{8,9},{9,10},{10,11},{12,13},{... | collective-permute-start | bytes 344072 | tf_op jit(solution)/shard_map/ppermute | solution.py:357
  18.5 0.0 copy-start.1
  18.5 9.2 %shard_map.47 = f32[16,16,256]{2,1,0:T(8,128)S(1)} custom-call(bf16[256,8192]{1,0:T(8,128)(2,1)S(1)} %get-tuple-element.9.weights, bf16[2,256,8192]{2,1,0:T(8,128)(2,1)S(1)} %get-tuple-element.10.ready, f32[16,4096]{1,0:T(8,128)S(1)} %get-tuple-element.11.partial, bf16[256,131072]{1,0:T(8,128)(2,1)} %volt.3), custom_call_target="tpu_custom_call" | custom-call | flops 7516192768 | bytes 29360128 | tf_op jit(solution)/shard_map/pallas_call | solution.py:262
  27.7 0.0 copy-done.1
  27.7 0.0 collective-permute-done
  27.8 18.4 %all_to_all.5 = bf16[16,2,16,256]{3,2,1,0:T(8,128)(2,1)S(1)} all-to-all(bf16[16,2,16,256]{3,2,1,0:T(8,128)(2,1)S(1)} %bitcast.9), channel_id=1, replica_groups=mesh['chan'=8,'wide'=2,'core'=2] {'chan','wide'}, dimensions={0} | all-to-all | bytes 524288 | tf_op jit(solution)/shard_map/all_to_all | solution.py:363
  46.2 0.0 collective-permute-start.1
  46.2 1.5 %collective-permute-done.1 = bf16[16,2,16,256]{3,2,1,0:T(8,128)(2,1)S(1)} collective-permute-done((bf16[16,2,16,256]{3,2,1,0:T(8,128)(2,1)S(1)}, bf16[16,2,16,256]{3,2,1,0:T(8,128)(2,1)S(1)}, u32[]{:S(2)}, u32[]{:S(2)}) %collective-permute-start.1) | collective-permute-done | bytes 262176 | tf_op jit(solution)/shard_map/ppermute | solution.py:364
  47.7 3.4 %shard_map.48 = bf16[512,2,2048]{2,1,0:T(2,128)(2,1)} custom-call(s32[1]{0:T(128)S(6)} %copy.5.offset.rotation, bf16[8,2,2,16,256]{4,3,2,1,0:T(8,128)(2,1)S(1)} %bitcast.7, bf16[8,2,2,16,256]{4,3,2,1,0:T(8,128)(2,1)S(1)} %bitcast.8), custom_call_target="tpu_custom_call" | custom-call | tf_op jit(solution)/shard_map/pallas_call | solution.py:319
  (3 shorter events, 0.1 us)
Async XLA Ops:
  0.7 1.0 %copy-start = (f32[8,8192]{1,0:T(8,128)S(1)}, f32[8,8192]{1,0:T(8,128)}, u32[]{:S(2)}) copy-start(f32[8,8192]{1,0:T(8,128)} %tap_ref.1) | copy-start | bytes 786436
  16.1 11.6 %collective-permute-start = (f32[16,7,256]{2,1,0:T(8,128)S(1)}, f32[16,7,256]{2,1,0:T(8,128)S(1)}, u32[]{:S(2)}, u32[]{:S(2)}) collective-permute-start(f32[16,7,256]{2,1,0:T(8,128)S(1)} %get-tuple-element.12), channel_id=1, source_target_pairs={{0,1},{1,2},{2,3},{4,5},{5,6},{6,7},{8,9},{9,10},{10,11},{12,13},{... | collective-permute-start | bytes 344072 | tf_op jit(solution)/shard_map/ppermute | solution.py:357
  18.5 9.2 %copy-start.1 = (s32[256,16]{0,1:T(8,128)S(1)}, s32[256,16]{0,1:T(8,128)}, u32[]{:S(2)}) copy-start(s32[256,16]{0,1:T(8,128)} %param.6) | copy-start | bytes 49156
  46.2 1.5 %collective-permute-start.1 = (bf16[16,2,16,256]{3,2,1,0:T(8,128)(2,1)S(1)}, bf16[16,2,16,256]{3,2,1,0:T(8,128)(2,1)S(1)}, u32[]{:S(2)}, u32[]{:S(2)}) collective-permute-start(bf16[16,2,16,256]{3,2,1,0:T(8,128)(2,1)S(1)} %all_to_all.5), channel_id=1, source_target_pairs={{0,1},{1,0},{2,3},{3,2},{4,5},{5,4},{6,7},{7,6},{8,9},{9,8},{10,11... | collective-permute-start | bytes 786440 | tf_op jit(solution)/shard_map/ppermute | solution.py:364

commit v7 on v6

--- a/solution.py
+++ b/solution.py
@@ -14,7 +14,7 @@
 DOWN = (((0,), (0,)), ((), ()))
 AHEAD = 3
 READY = 2
-LATE = 9
+LATE = 10
 
 
 def channel_table(frame, channels, width, shift):

time: 51.4 us -> 51.3 us (level)
    pallas_call x1, Pallas kernels: 9.22 us -> 7.93 us  [filterbank(): pl.pallas_call(functools.partial(early_kernel, spec, rows), in_specs=[vme...]
    pallas_call x1, Pallas kernels: 14.5 us -> 15.7 us  [filterbank(): pl.pallas_call(functools.partial(late_kernel, spec, rows), in_specs=[pl.B...]
  transfers between devices with their start and end apart: 2 -> 2, of which waited for: 1 -> 1; matrix products, arithmetic and copies ran while one was open for 0% -> 0% of each run, Pallas kernels for 18% -> 16%
where the time goes in v7:
time: 51.3 us; the launch traced here: 51.1 us
  Pallas kernels  27.1 us (53%)
  blocking collectives  18.4 us (36%)
  starting transfers between devices  2.37 us (5%)
  waiting for transfers between devices  1.54 us (3%)
  local copies, waits for them, and re-layouts  0.97 us (2%)
  between operations  0.73 us (1%)
    all_to_all x1, blocking collectives, shards(): lax.all_to_all(sent, ('chan', 'wide'), split_axis=0, concat_axis=0, tiled...  18.4 us
    pallas_call x1, Pallas kernels, filterbank(): pl.pallas_call(functools.partial(late_kernel, spec, rows), in_specs=[pl.B...  15.7 us
    pallas_call x1, Pallas kernels, filterbank(): pl.pallas_call(functools.partial(early_kernel, spec, rows), in_specs=[vme...  7.93 us
    pallas_call x1, Pallas kernels, correlate(): pl.pallas_call(functools.partial(correlate_kernel, scale), grid_spec=pltp...  3.44 us
    ppermute x1, starting transfers between devices, shards(): lax.ppermute(tail, ('wide', 'core'), [(i, i + 1) for i in range(time_coun...  2.36 us
    ppermute x1, waiting for transfers between devices, shards(): other = lax.ppermute(mine, 'core', [(0, 1), (1, 0)])  1.53 us
  transfers between devices with their start and end apart: 2, of which 1 were waited for; matrix products, arithmetic and copies ran while one was open for 0% of the time, Pallas kernels for 16%

profile of v7, /device:TPU:0, one launch (start us, length us, event | category | flops | bytes accessed | tf_op | source)
XLA Modules:
  0.0 51.1 jit_solution(7817836004258427090)
XLA Ops:
  0.7 0.0 copy-start
  0.7 0.9 %copy-done = f32[8,8192]{1,0:T(8,128)S(1)} copy-done((f32[8,8192]{1,0:T(8,128)S(1)}, f32[8,8192]{1,0:T(8,128)}, u32[]{:S(2)}) %copy-start) | copy-done | bytes 262168
  1.6 15.7 %shard_map.46 = (f32[16,7,256]{2,1,0:T(8,128)S(1)}, f32[16,4096]{1,0:T(8,128)S(1)}, bf16[256,8192]{1,0:T(8,128)(2,1)S(1)}, bf16[2,256,8192]{2,1,0:T(8,128)(2,1)S(1)}) custom-call(s32[1]{0:T(128)S(6)} %copy.5.offset.rotation, f32[8,8192]{1,0:T(8,128)S(1)} %copy-done, bf16[256,131072]{1,0:T(8,128)(2,1)} %volt.3), custom_call_target="tpu_custom_call" | custom-call | flops 10737418240 | bytes 41943040 | tf_op jit(solution)/shard_map/pallas_call | solution.py:243
  17.3 2.4 %collective-permute-start = (f32[16,7,256]{2,1,0:T(8,128)S(1)}, f32[16,7,256]{2,1,0:T(8,128)S(1)}, u32[]{:S(2)}, u32[]{:S(2)}) collective-permute-start(f32[16,7,256]{2,1,0:T(8,128)S(1)} %get-tuple-element.12), channel_id=1, source_target_pairs={{0,1},{1,2},{2,3},{4,5},{5,6},{6,7},{8,9},{9,10},{10,11},{12,13},{... | collective-permute-start | bytes 344072 | tf_op jit(solution)/shard_map/ppermute | solution.py:357
  19.7 0.0 copy-start.1
  19.7 7.9 %shard_map.47 = f32[16,16,256]{2,1,0:T(8,128)S(1)} custom-call(bf16[256,8192]{1,0:T(8,128)(2,1)S(1)} %get-tuple-element.9.weights, bf16[2,256,8192]{2,1,0:T(8,128)(2,1)S(1)} %get-tuple-element.10.ready, f32[16,4096]{1,0:T(8,128)S(1)} %get-tuple-element.11.partial, bf16[256,131072]{1,0:T(8,128)(2,1)} %volt.3), custom_call_target="tpu_custom_call" | custom-call | flops 6442450944 | bytes 25165824 | tf_op jit(solution)/shard_map/pallas_call | solution.py:262
  27.6 0.0 copy-done.1
  27.6 0.0 collective-permute-done
  27.7 18.4 %all_to_all.5 = bf16[16,2,16,256]{3,2,1,0:T(8,128)(2,1)S(1)} all-to-all(bf16[16,2,16,256]{3,2,1,0:T(8,128)(2,1)S(1)} %bitcast.9), channel_id=1, replica_groups=mesh['chan'=8,'wide'=2,'core'=2] {'chan','wide'}, dimensions={0} | all-to-all | bytes 524288 | tf_op jit(solution)/shard_map/all_to_all | solution.py:363
  46.1 0.0 collective-permute-start.1
  46.1 1.5 %collective-permute-done.1 = bf16[16,2,16,256]{3,2,1,0:T(8,128)(2,1)S(1)} collective-permute-done((bf16[16,2,16,256]{3,2,1,0:T(8,128)(2,1)S(1)}, bf16[16,2,16,256]{3,2,1,0:T(8,128)(2,1)S(1)}, u32[]{:S(2)}, u32[]{:S(2)}) %collective-permute-start.1) | collective-permute-done | bytes 262176 | tf_op jit(solution)/shard_map/ppermute | solution.py:364
  47.6 3.4 %shard_map.48 = bf16[512,2,2048]{2,1,0:T(2,128)(2,1)} custom-call(s32[1]{0:T(128)S(6)} %copy.5.offset.rotation, bf16[8,2,2,16,256]{4,3,2,1,0:T(8,128)(2,1)S(1)} %bitcast.7, bf16[8,2,2,16,256]{4,3,2,1,0:T(8,128)(2,1)S(1)} %bitcast.8), custom_call_target="tpu_custom_call" | custom-call | tf_op jit(solution)/shard_map/pallas_call | solution.py:319
  (3 shorter events, 0.1 us)
Async XLA Ops:
  0.7 1.0 %copy-start = (f32[8,8192]{1,0:T(8,128)S(1)}, f32[8,8192]{1,0:T(8,128)}, u32[]{:S(2)}) copy-start(f32[8,8192]{1,0:T(8,128)} %tap_ref.1) | copy-start | bytes 786436
  17.3 10.3 %collective-permute-start = (f32[16,7,256]{2,1,0:T(8,128)S(1)}, f32[16,7,256]{2,1,0:T(8,128)S(1)}, u32[]{:S(2)}, u32[]{:S(2)}) collective-permute-start(f32[16,7,256]{2,1,0:T(8,128)S(1)} %get-tuple-element.12), channel_id=1, source_target_pairs={{0,1},{1,2},{2,3},{4,5},{5,6},{6,7},{8,9},{9,10},{10,11},{12,13},{... | collective-permute-start | bytes 344072 | tf_op jit(solution)/shard_map/ppermute | solution.py:357
  19.7 8.0 %copy-start.1 = (s32[256,16]{0,1:T(8,128)S(1)}, s32[256,16]{0,1:T(8,128)}, u32[]{:S(2)}) copy-start(s32[256,16]{0,1:T(8,128)} %param.6) | copy-start | bytes 49156
  46.1 1.5 %collective-permute-start.1 = (bf16[16,2,16,256]{3,2,1,0:T(8,128)(2,1)S(1)}, bf16[16,2,16,256]{3,2,1,0:T(8,128)(2,1)S(1)}, u32[]{:S(2)}, u32[]{:S(2)}) collective-permute-start(bf16[16,2,16,256]{3,2,1,0:T(8,128)(2,1)S(1)} %all_to_all.5), channel_id=1, source_target_pairs={{0,1},{1,0},{2,3},{3,2},{4,5},{5,4},{6,7},{7,6},{8,9},{9,8},{10,11... | collective-permute-start | bytes 786440 | tf_op jit(solution)/shard_map/ppermute | solution.py:364
